TPU v7x, 32 devices: a whole 2x2x4 slice. The times are simulated.
32 devices in a mesh: dp: 8 (over z, y), tensor: 4 (over x, core).
Axes of the slice: x: 2, y: 2, z: 4, core: 2. Of those that a mesh axis runs over, the one named last changes fastest.
Arguments:
- lang_in: bfloat16 [3840, 768], P(('dp', 'tensor')), may hold values from -6 to 6
- visn_in: bfloat16 [6912, 768], P(('dp', 'tensor')), may hold values from -6 to 6
- word_len: int32 [192], P(('dp', 'tensor')), may hold values from 5 to 20, as said below
- lang_cot: bfloat16 [3840, 768], P(('dp', 'tensor')), may hold values from -6 to 6
- visn_cot: bfloat16 [6912, 768], P(('dp', 'tensor')), may hold values from -6 to 6
- att_in: float32 [3, 768, 3, 768], P(None, 'dp', None, 'tensor'), may hold values from -0.21875 to 0.21875
- att_out: float32 [3, 768, 768], P(None, 'tensor', 'dp'), may hold values from -0.875 to 0.875
- ffn_up: float32 [2, 768, 3072], P(None, 'dp', 'tensor'), may hold values from -0.21875 to 0.21875
- ffn_down: float32 [2, 3072, 768], P(None, 'tensor', 'dp'), may hold values from -0.109375 to 0.109375
- vectors: float32 [21, 768], replicated, as said below
- ffn_bias1: float32 [2, 3072], replicated, may hold values from -3 to 3
- att_in_m: float32 [3, 768, 3, 768], P(None, 'dp', None, 'tensor'), may hold values from -192 to 192
- att_in_v: float32 [3, 768, 3, 768], P(None, 'dp', None, 'tensor'), may hold values from 967.68 to 3870.72
- att_out_m: float32 [3, 768, 768], P(None, 'tensor', 'dp'), may hold values from -192 to 192
- att_out_v: float32 [3, 768, 768], P(None, 'tensor', 'dp'), may hold values from 967.68 to 3870.72
- ffn_up_m: float32 [2, 768, 3072], P(None, 'dp', 'tensor'), may hold values from -128 to 128
- ffn_up_v: float32 [2, 768, 3072], P(None, 'dp', 'tensor'), may hold values from 430.08 to 1720.32
- ffn_down_m: float32 [2, 3072, 768], P(None, 'tensor', 'dp'), may hold values from -256 to 256
- ffn_down_v: float32 [2, 3072, 768], P(None, 'tensor', 'dp'), may hold values from 1720.32 to 6881.28
- vectors_m: float32 [21, 768], replicated, may hold values from -448 to 448
- vectors_v: float32 [21, 768], replicated, may hold values from 5268.48 to 21073.92
- bias1_m: float32 [2, 3072], replicated, may hold values from -128 to 128
- bias1_v: float32 [2, 3072], replicated, may hold values from 430.08 to 1720.32
Outputs:
- lang_out: float32 [3840, 768], P(('dp', 'tensor'))
- visn_out: float32 [6912, 768], P(('dp', 'tensor'))
- lang_grad: float32 [3840, 768], P(('dp', 'tensor'))
- visn_grad: float32 [6912, 768], P(('dp', 'tensor'))
- att_in_grad: float32 [3, 768, 3, 768], P(None, 'dp', None, 'tensor')
- att_in_m_new: float32 [3, 768, 3, 768], P(None, 'dp', None, 'tensor')
- att_in_v_new: float32 [3, 768, 3, 768], P(None, 'dp', None, 'tensor')
- att_in_new: float32 [3, 768, 3, 768], P(None, 'dp', None, 'tensor')
- att_in_copy: bfloat16 [3, 768, 3, 768], P(None, 'dp', None, 'tensor')
- att_out_grad: float32 [3, 768, 768], P(None, 'tensor', 'dp')
- att_out_m_new: float32 [3, 768, 768], P(None, 'tensor', 'dp')
- att_out_v_new: float32 [3, 768, 768], P(None, 'tensor', 'dp')
- att_out_new: float32 [3, 768, 768], P(None, 'tensor', 'dp')
- att_out_copy: bfloat16 [3, 768, 768], P(None, 'tensor', 'dp')
- ffn_up_grad: float32 [2, 768, 3072], P(None, 'dp', 'tensor')
- ffn_up_m_new: float32 [2, 768, 3072], P(None, 'dp', 'tensor')
- ffn_up_v_new: float32 [2, 768, 3072], P(None, 'dp', 'tensor')
- ffn_up_new: float32 [2, 768, 3072], P(None, 'dp', 'tensor')
- ffn_up_copy: bfloat16 [2, 768, 3072], P(None, 'dp', 'tensor')
- ffn_down_grad: float32 [2, 3072, 768], P(None, 'tensor', 'dp')
- ffn_down_m_new: float32 [2, 3072, 768], P(None, 'tensor', 'dp')
- ffn_down_v_new: float32 [2, 3072, 768], P(None, 'tensor', 'dp')
- ffn_down_new: float32 [2, 3072, 768], P(None, 'tensor', 'dp')
- ffn_down_copy: bfloat16 [2, 3072, 768], P(None, 'tensor', 'dp')
- vectors_grad: float32 [21, 768], replicated
- vectors_m_new: float32 [21, 768], replicated
- vectors_v_new: float32 [21, 768], replicated
- vectors_new: float32 [21, 768], replicated
- bias1_grad: float32 [2, 3072], replicated
- bias1_m_new: float32 [2, 3072], replicated
- bias1_v_new: float32 [2, 3072], replicated
- bias1_new: float32 [2, 3072], replicated
Inputs may be any that keep to these rules, and one draw needn't show every extreme that they name: Each item has 20 word slots, of which the first word_len are words; some item has all 20. `vectors`: rows 3, 8, 13, 16 and 19 are layer norms' gains, positive; the other rows are biases and shifts.
All inputs are finite; a program needn't handle non-finite values.
Results may differ from a plain program's by a relative error of at most 0.033.
Values may be sent and summed in bfloat16 or wider, within the bound.
No kernel may reach another device: no remote copies, remote signals or barrier semaphores. Data moves between devices by JAX's collectives and lax.ppermute only.
A program may use at most 128 MiB of HBM per device.

v0:
```python
import functools

import jax
import jax.numpy as jnp
from jax import lax
from jax.experimental import pallas as pl
from jax.experimental.pallas import tpu as pltpu
from jax.sharding import PartitionSpec as P

HD = 64
LW = 20
STEP = 10

lnorm_eps = 1e-12
decay_one = 0.5
decay_two = 0.5
adam_eps = 1e-08
weight_decay = 0.01
rate_in = 0.03
rate_out = 0.1
rate_up = 0.03
rate_down = 0.015
rate_vector = 0.2
rate_bias = 0.2

F32 = jnp.float32
BF16 = jnp.bfloat16
HIGHEST = lax.Precision.HIGHEST

def tie(value, after):
    return lax.optimization_barrier((value, after))[0]


def listed(*values):
    return jax.tree.leaves(values)


class Plain:
    def __init__(self, mesh):
        self.n_dp, self.n_t = mesh.shape["dp"], mesh.shape["tensor"]
        self.groups = 1

    def row_blocks(self):
        return jnp.arange(self.n_dp, dtype=jnp.int32)

    def piece_at(self, j):
        return jnp.int32(j)

    def gather(self, shard):
        whole = lax.all_gather(shard, "dp", axis=0)[:, None]
        for_all = lax.all_gather(whole, "tensor", axis=0)
        return [[(for_all[j], 0)] for j in range(self.n_t)]

    def first(self, shards):
        return (), {"a0": self.gather(shards["a0"])}

    def begin(self, pair, shards, after):
        return {name: self.gather(shards[name]) for name in pair}

    def begin_late(self, pair, shards):
        return self.begin(pair, shards, ())

    def gather_late(self, state, after):
        return state

    def complete_late(self, state, after):
        return state

    def swap_late(self, state, after):
        return state

    def begun(self, state):
        return ()

    def complete(self, state, after):
        return state

    def swap_out(self, stash):
        return list(stash)

    def fold(self, items, after=()):
        stashes, kinds = weight_kinds(items)
        outs = [shape((self.n_t, stashes[0].shape[2], stashes[0].shape[2]), BF16)] * len(items)
        return small(functools.partial(grad_plain_kernel, kinds, self.n_t), stashes, outs, 8, 40, after)

    def fold_wide(self, items, after=()):
        return self.fold(items, after)

    def send(self, state, after=()):
        return state

    def bump(self, *states, after=()):
        return list(states)

    def merge_and_bump(self, state, *others, after=()):
        return [state, *others]

    def go(self, state, after=()):
        return state

    def landed(self, state):
        return ()

    def merge(self, state, after=()):
        return state

    def rest(self, shares):
        return shares

    def over_z(self, state, after=()):
        out = []
        for full in state:
            mine = lax.psum_scatter(full, "tensor", scatter_dimension=0)
            out.append(lax.psum_scatter(mine, "dp", scatter_dimension=0, tiled=True))
        return out

    def gate(self, state):
        return []

    def first_totals(self, value):
        return lax.psum(value, ("dp", "tensor"))

    def next_total(self, value, axis, after):
        return value


class Grid:
    def __init__(self, mesh):
        self.n_dp, self.n_t = mesh.shape["dp"], mesh.shape["tensor"]
        self.groups = 2
        self.z_groups = [[z * 2 + y for z in range(4)] for y in range(2)]

    def row_blocks(self):
        y = lax.axis_index("dp") % 2
        return jnp.stack([2 * z + (y ^ k) for k in range(2) for z in range(4)])

    def piece_at(self, j):
        return lax.axis_index("tensor") ^ j

    def swap(self, value, axis, mask):
        size = self.n_dp if axis == "dp" else self.n_t
        return lax.ppermute(value, axis, [(i, i ^ mask) for i in range(size)])

    def over_x(self, value):
        return self.swap(value, "tensor", 2)

    def over_core(self, value):
        return self.swap(value, "tensor", 1)

    def over_y(self, value):
        return self.swap(value, "dp", 1)

    def z_gather(self, value):
        z = lax.axis_index("dp") // 2
        out = jnp.zeros((4,) + value.shape, value.dtype)
        out = lax.dynamic_update_slice_in_dim(out, value[None], z, 0)
        near = self.swap(value, "dp", 2)
        out = lax.dynamic_update_slice_in_dim(out, near[None], z ^ 1, 0)
        for m in range(2, 4):
            out = lax.dynamic_update_slice_in_dim(out, self.swap(value, "dp", 2 * m)[None], z ^ m, 0)
        return out, near

    def z_scatter(self, value, after):
        z = lax.axis_index("dp") // 2
        total = lax.dynamic_index_in_dim(value, z, 0, keepdims=False).astype(F32)
        parts = [lax.dynamic_index_in_dim(value, z ^ m, 0, keepdims=False) for m in range(1, 4)]
        for part in tie([self.swap(part, "dp", 2 * m) for m, part in enumerate(parts, 1)], after):
            total = total + part.astype(F32)
        return total.astype(BF16)

    def first(self, shards):
        s, near = self.z_gather(shards["a0"][None])
        u, t = self.over_x(s), self.over_y(s)
        half = s.shape[-1] // 2
        v = jnp.concatenate([self.over_x(t[..., :half]), self.over_y(u[..., half:])], axis=-1)
        mine = (s, t, u, v)
        other = [self.over_core(k) for k in mine]
        return near, {"a0": [[(k[0], 0), (k[1], 0)] if j < 2 else [(k[2], 0), (k[3], 0)] for j, k in enumerate((mine, other, mine, other))]}

    def begin(self, pair, shards, after):
        s = lax.all_gather(jnp.stack([shards[n] for n in pair]), "dp", axis=0, axis_index_groups=self.z_groups)
        s = tie(s, after)
        return pair, s, self.over_x(s), self.over_y(s)

    def begin_late(self, pair, shards):
        first, second = shards[pair[0]], shards[pair[1]]
        blocks = jnp.stack([first, self.over_x(first), second, self.over_y(second)])
        return pair, blocks

    def gather_late(self, state, after):
        pair, blocks = state
        return pair, lax.all_gather(tie(blocks, after), "dp", axis=0, axis_index_groups=self.z_groups)

    def complete_late(self, state, after):
        pair, held = state
        cut = tie(held, after)
        return pair, held, self.over_y(cut[:, :2]), self.over_x(cut[:, 2:])

    def swap_late(self, state, after):
        pair, mine = state[0], state[1:]
        other = [self.over_core(mine[0])] + [self.over_core(k) for k in tie(mine[1:], after)]
        out = {pair[0]: [], pair[1]: []}
        for x in range(2):
            for k in (mine, other):
                out[pair[0]].append([(k[0], x), (k[1], x)])
                out[pair[1]].append([(k[2 * x], 2 - 2 * x), (k[2 * x], 3 - 2 * x)])
        return out

    def begun(self, state):
        return state[3:]

    def complete(self, state, after):
        pair, s, u, t = state
        cut_t, cut_u = tie((t, u), after)
        v0, v1 = self.over_x(cut_t[:, 0:1]), self.over_y(cut_u[:, 1:2])
        mine = (s, t, u, v0, v1)
        other = [self.over_core(k) for k in mine]
        out = {}
        for m, name in enumerate(pair):
            out[name] = [
                [(k[0], m), (k[1], m)] if j < 2 else [(k[2], m), (k[3 + m], 0)] for j, k in enumerate((mine, other, mine, other))
            ]
        return out

    def swap_out(self, stash):
        keep, send = stash
        return [keep, self.over_core(send)]

    def fold(self, items, after=()):
        stashes, kinds = weight_kinds(items)
        n, cols = len(items), stashes[0].shape[2]
        half = cols // 2
        cut = cols if n == 2 else cols // 2
        outs = (shape((n, half, cols), BF16),) * 3 + (shape((half, cut), BF16),) * 2
        s, t, u, va, vb = small(functools.partial(grad_kernel, kinds, 2), stashes, outs, 3, 30, after)
        return s, t, u, va, vb

    def fold_wide(self, items, after=()):
        stashes, kinds = weight_kinds(items)
        half, cols = stashes[0].shape[2] // 2, stashes[0].shape[2]
        outs = [shape((n, half, cols), BF16) for n in (4, 2, 2)]
        keep, ty, tx = small(functools.partial(grad_wide_kernel, kinds, 2), stashes, outs, 3, 30, after)
        return keep, self.over_y(ty), self.over_x(tx), None

    def send(self, state, after=()):
        s, t, u, va, vb = state
        va, vb = tie((va, vb), after)
        return s, t, u, self.over_x(va), self.over_y(vb)

    def bump_spec(self, state, after=()):
        s, t, u, ra, rb = state
        t, u = tie((t, u), after)
        return bump_kernel, [t, u, ra, rb], [shape(t.shape, BF16), shape(u.shape, BF16)]

    def bump(self, *states, after=()):
        done = several([self.bump_spec(k, after) for k in states], 1.5 * len(states))
        return [(k[0], t, u) for k, (t, u) in zip(states, done)]

    def merge_spec(self, state, after=()):
        s, rt, ru, wide = state
        n, half, cols = s.shape
        if wide is None:
            return close_wide_kernel, [tie(s, after), rt, ru], [shape((4, 4, half // 4, cols), BF16)]
        return close_kernel, [tie(s, after), rt, ru], [shape((4, n, half // 4, cols), BF16)]

    def merge_and_bump(self, state, *others, after=()):
        done = several([self.merge_spec(state, after)] + [self.bump_spec(k, after) for k in others], 1.5 + 1.5 * len(others))
        return [done[0][0]] + [(k[0], t, u) for k, (t, u) in zip(others, done[1:])]

    def go(self, state, after=()):
        s, t, u = state
        cut_t, cut_u = tie((t, u), after)
        return s, self.over_y(cut_t), self.over_x(cut_u), t

    def landed(self, state):
        return state[1:3]

    def merge(self, state, after=()):
        return several([self.merge_spec(state, after)], 1.5)[0][0]

    def over_z(self, both, after=()):
        if both.shape[1] == 1:
            return self.z_scatter(both, after)
        return lax.psum_scatter(both, "dp", scatter_dimension=0, axis_index_groups=self.z_groups)

    def rest(self, held):
        if held.shape[0] == 4:
            return [held[0] + self.over_x(held[1]), held[2] + self.over_y(held[3])]
        return [held[i] for i in range(held.shape[0])]

    def gate(self, state):
        if not isinstance(state, tuple):
            return [state]
        if len(state) == 4:
            return [state[0] if state[3] is None else state[3]]
        return [state[1] if len(state) == 3 else state[0]]

    def first_totals(self, value):
        for axis, mask in (("tensor", 1), ("dp", 2), ("dp", 4)):
            value = value + self.swap(value, axis, mask)
        return value

    def next_total(self, value, axis, after):
        value = tie(value, after)
        return value + (self.over_x(value) if axis == "x" else self.over_y(value))


def adam_step(weight, gradient, first, second, rate):
    first_new = decay_one * first + (1.0 - decay_one) * gradient
    second_new = decay_two * second + (1.0 - decay_two) * gradient * gradient
    fix_one = 1.0 - decay_one**STEP
    fix_two = 1.0 - decay_two**STEP
    ratio = first_new / fix_one / (jnp.sqrt(second_new / fix_two) + adam_eps)
    return (first_new, second_new, weight - rate * (ratio + weight_decay * weight))


def mm(left, right):
    return jnp.dot(left, right, preferred_element_type=F32)


def mm_nt(left, right):
    return lax.dot_general(left, right, (((1,), (1,)), ((), ())), preferred_element_type=F32)


def mm_tn(left, right):
    return lax.dot_general(left, right, (((0,), (0,)), ((), ())), preferred_element_type=F32)


def normed(z, gain, shift):
    centered = z - jnp.mean(z, axis=-1, keepdims=True)
    scale = lax.rsqrt(jnp.mean(centered * centered, axis=-1, keepdims=True) + lnorm_eps)
    xhat = centered * scale
    return xhat * gain + shift, xhat, scale


def norm_back(g, xhat, scale, gain, sums_ref):
    gg = g * gain
    g_z = (gg - jnp.mean(gg, axis=-1, keepdims=True) - xhat * jnp.mean(gg * xhat, axis=-1, keepdims=True)) * scale
    sums_ref[...] = jnp.zeros(sums_ref.shape, F32)
    sums_ref[0:1, :] = jnp.sum(g_z, axis=0, keepdims=True)
    sums_ref[1:2, :] = jnp.sum(g * xhat, axis=0, keepdims=True)
    sums_ref[2:3, :] = jnp.sum(g, axis=0, keepdims=True)
    return g_z


def put_adam(refs, at, gradient, rate):
    w_ref, m_ref, v_ref, g_out, m_out, v_out, w_out, copy_out = refs
    m_new, v_new, w_new = adam_step(w_ref[at], gradient, m_ref[at], v_ref[at], rate)
    g_out[at], m_out[at], v_out[at], w_out[at] = gradient, m_new, v_new, w_new
    copy_out[at] = w_new.astype(BF16)


def adam_ffn_kernel(ins, outs, up_ref, down_ref):
    put_adam(ins[:3] + outs[:5], 0, up_ref[...].astype(F32), rate_up)
    put_adam(ins[3:] + outs[5:], 0, down_ref[...].astype(F32), rate_down)


def adam_att_kernel(ins, outs, share_ref):
    g = share_ref[...].astype(F32)
    cols = ins[0].shape[3]
    for i in range(3):
        put_adam(ins[:3] + outs[:5], (0, i), g[:, i * cols : (i + 1) * cols], rate_in)
    put_adam(ins[3:] + outs[5:], 0, g[:, 3 * cols :].T, rate_out)


def adam_call(kernel, at, shares, groups, earlier):
    flat_in = [a for g in groups for a in g]

    def one(a):
        return pl.BlockSpec((1,) + a.shape[1:], lambda i: at + (0,) * (len(a.shape) - 1))

    outs = []
    for g in groups:
        outs += [shape(g[0].shape)] * 4 + [shape(g[0].shape, BF16)]
    n, n_in, old = len(shares), len(flat_in), list(earlier or ())

    def body(*refs):
        kernel(refs[n : n + n_in], refs[n + n_in + len(old) :], *refs[:n])

    return pl.pallas_call(
        body,
        grid=(1,),
        in_specs=[pl.BlockSpec(a.shape, lambda i: (0, 0)) for a in shares] + [one(a) for a in flat_in] + [pl.BlockSpec(memory_space=pl.ANY)] * len(old),
        out_specs=tuple(one(o) for o in outs),
        out_shape=tuple(outs),
        input_output_aliases={n + n_in + i: i for i in range(len(old))},
        cost_estimate=work(3),
        compiler_params=pltpu.CompilerParams(vmem_limit_bytes=24 * MIB),
    )(*shares, *flat_in, *old)


def head_lanes(hn, width):
    lane = lax.broadcasted_iota(jnp.int32, (1, width), 1) // HD
    return [lane == h for h in range(hn)]


def stacked(value, lanes):
    return jnp.concatenate([jnp.where(m, value, 0.0) for m in lanes], axis=0).astype(BF16)


def gathered(value, lanes):
    rows = value.shape[0] // len(lanes)
    parts = [jnp.where(m, value[h * rows : (h + 1) * rows], 0.0) for h, m in enumerate(lanes)]
    return sum(parts[1:], parts[0])


def probabilities(q_rows, k, mask):
    rows = mask.shape[0]
    s = mm_nt(q_rows, k).reshape(-1, rows, rows) * HD ** (-0.5)
    s = jnp.where(mask[None] > 0, s, -1e30)
    e = jnp.exp(s - jnp.max(s, axis=-1, keepdims=True))
    return (e / jnp.sum(e, axis=-1, keepdims=True)).reshape(-1, rows)


def att_fwd_kernel(n, nw, hn, x_ref, mask_ref, bias_ref, vec_ref, *refs):
    w, (out_ref, xhat_ref, scale_ref, qkv_ref, mix_ref) = split(refs[:nw], n), refs[nw:]
    c, lanes = hn * HD, head_lanes(hn, 256)
    x = x_ref[...]
    x16 = x.astype(BF16)
    z = x + vec_ref[0:1, :]
    for j in range(n):
        blank = jnp.zeros((1, c), F32)
        bias = jnp.concatenate([bias_ref[0:1, j * c : (j + 1) * c], blank, bias_ref[1:2, j * c : (j + 1) * c], blank], axis=1)
        qkv = times(x16, w[j]) + bias
        k = pltpu.roll(qkv[:, c - 64 : c + 192], 192, 1).astype(BF16)
        q, v = qkv[:, :256].astype(BF16), qkv[:, 2 * c : 2 * c + 256].astype(BF16)
        qkv_ref[j, :, :256], qkv_ref[j, :, 256:512], qkv_ref[j, :, 512:] = q, k, v
        p = probabilities(stacked(q.astype(F32), lanes), k, mask_ref[...]).astype(BF16)
        mix = pltpu.roll(gathered(mm(p, v), lanes), 64, 1).astype(BF16)
        mix_ref[j] = mix
        z = z + times_t(mix, w[j], 3 * c - 64)
    out, xhat, scale = normed(z, vec_ref[1:2, :], vec_ref[2:3, :])
    out_ref[...] = out
    xhat_ref[...] = xhat
    scale_ref[...] = jnp.broadcast_to(scale, scale_ref.shape)


def att_bwd_kernel(n, nw, hn, g_ref, x_ref, mask_ref, vec_ref, xhat_ref, scale_ref, qkv_ref, mix_ref, *refs):
    w, (gin_ref, sums_ref, bias_ref), stash = split(refs[:nw], n), refs[nw : nw + 3], refs[nw + 3 :]
    c, lanes, groups = hn * HD, head_lanes(hn, 256), len(stash)
    g_z = norm_back(g_ref[...], xhat_ref[...], scale_ref[:, 0:1], vec_ref[1:2, :], sums_ref)
    wide, x16 = g_z.astype(BF16), x_ref[...].astype(BF16)
    for ref in stash:
        ref[0], ref[1] = x16, wide
    gin = g_z
    for j in range(n):
        q, k, v = qkv_ref[j, :, :256], qkv_ref[j, :, 256:512], qkv_ref[j, :, 512:]
        d_mix = pltpu.roll(times_from(wide, w[j], 3 * c - 64), 192, 1).astype(BF16)
        da, q = stacked(d_mix.astype(F32), lanes), stacked(q.astype(F32), lanes)
        p = probabilities(q, k, mask_ref[...])
        dv = mm_tn(p.astype(BF16), da)
        dp = mm_nt(da, v)
        ds = (p * (dp - jnp.sum(p * dp, axis=-1, keepdims=True))).astype(BF16) * HD ** (-0.5)
        dq = gathered(mm(ds, k), lanes)
        dk = pltpu.roll(mm_tn(ds, q), 64, 1)
        front = [dq[:, :128], dq[:, 128:] + dk[:, :128], dk[:, 128:], dv[:, :128]]
        d_qkv = jnp.concatenate(front + [dv[:, 128:]], axis=1).astype(BF16)
        sums = jnp.sum(d_qkv.astype(F32), axis=0, keepdims=True)
        bias_ref[0:1, j * c : (j + 1) * c] = sums[:, :c]
        bias_ref[1:2, j * c : (j + 1) * c] = sums[:, 2 * c : 3 * c]
        place = stash[j % groups].at[2 + j // groups]
        place[:, :512] = d_qkv[:, :512]
        place[:, 512:640] = d_qkv[:, 512:] + mix_ref[j, :, :128]
        place[:, 640:] = mix_ref[j, :, 128:]
        gin = gin + times_t(d_qkv, w[j], 0, 640)
    gin_ref[...] = gin


def ffn_kernel(n, nw, x_ref, cot_ref, bias_ref, vec_ref, *refs):
    up, down = split(refs[:nw], n), split(refs[nw : 2 * nw], n)
    out_ref, gin_ref, sums_ref, dbias_ref = refs[2 * nw : 2 * nw + 4]
    slope_ref, stash = refs[-1], refs[2 * nw + 4 : -1]
    groups, held = len(stash), n // len(stash)
    x = x_ref[...]
    x16 = x.astype(BF16)
    z = x + vec_ref[0:1, :]
    for j in range(n):
        inner = times(x16, up[j]) + bias_ref[j : j + 1, :]
        half = 0.5 * (1.0 + lax.erf(inner * 0.7071067811865476))
        act = (inner * half).astype(BF16)
        slope_ref[j] = half + inner * (0.3989422804014327 * jnp.exp(-0.5 * inner * inner))
        stash[j % groups][2 + j // groups] = act
        z = z + times_t(act, down[j])
    out, xhat, scale = normed(z, vec_ref[1:2, :], vec_ref[2:3, :])
    out_ref[...] = out
    g_z = norm_back(cot_ref[...].astype(F32), xhat, scale, vec_ref[1:2, :], sums_ref)
    wide = g_z.astype(BF16)
    for ref in stash:
        ref[0], ref[1] = x16, wide
    gin = g_z
    for j in range(n):
        d_inner = (times(wide, down[j]) * slope_ref[j]).astype(BF16)
        dbias_ref[j : j + 1, :] = jnp.sum(d_inner.astype(F32), axis=0, keepdims=True)
        stash[j % groups][2 + held + j // groups] = d_inner
        gin = gin + times_t(d_inner, up[j])
    gin_ref[...] = gin


def weight_grad(kind, refs, i, held):
    total = None
    for ref in refs:
        if kind == "d":
            part = mm_tn(ref[1], ref[2 + i])
        elif kind == "u":
            part = mm_tn(ref[0], ref[2 + held + i])
        else:
            both = ref[2 + i]
            part = mm_tn(ref[0], both)
            tail = mm_tn(ref[1], both[:, 512:])
            own = lax.broadcasted_iota(jnp.int32, (1, 256), 1) < 64
            part = jnp.concatenate([part[:, :512], jnp.where(own, part[:, 512:], tail)], axis=1)
        total = part if total is None else total + part
    return total.astype(BF16)


def grad_kernel(kinds, held, *refs):
    outs = refs[-5:]
    s_ref, t_ref, u_ref, va_ref, vb_ref = outs
    for m, (kind, at) in enumerate(kinds):
        g = weight_grad(kind, [refs[i] for i in at], 1, held)
        half = g.shape[0] // 2
        u_ref[m], v = g[:half], g[half:]
        if len(kinds) == 1:
            va_ref[...], vb_ref[...] = v[:, : v.shape[1] // 2], v[:, v.shape[1] // 2 :]
        elif m == 0:
            va_ref[...] = v
        else:
            vb_ref[...] = v
        g = weight_grad(kind, [refs[i] for i in at], 0, held)
        s_ref[m], t_ref[m] = g[:half], g[half:]


def grad_wide_kernel(kinds, held, *refs):
    keep_ref, y_ref, x_ref = refs[-3:]
    for m, (kind, at) in enumerate(kinds):
        for x in range(2):
            g = weight_grad(kind, [refs[i] for i in at], x, held)
            half = g.shape[0] // 2
            if m == 0:
                keep_ref[x], y_ref[x] = g[:half], g[half:]
            else:
                for y in range(2):
                    out = keep_ref.at[2 + y] if x == 0 else x_ref.at[y]
                    out[...] = g[y * half : (y + 1) * half]


def close_wide_kernel(keep_ref, y_ref, x_ref, out_ref):
    rows = keep_ref.shape[1] // 4
    for b in range(4):
        for z in range(4):
            at = slice(z * rows, (z + 1) * rows)
            other = y_ref[b, at] if b < 2 else x_ref[b - 2, at]
            out_ref[z, b] = (keep_ref[b, at].astype(F32) + other.astype(F32)).astype(BF16)


def grad_plain_kernel(kinds, held, *refs):
    for m, (kind, at) in enumerate(kinds):
        for i in range(held):
            refs[len(refs) - len(kinds) + m][i] = weight_grad(kind, [refs[k] for k in at], i, held)


def bump_kernel(t_ref, u_ref, a_ref, b_ref, t_out, u_out):
    cut, cols, last = a_ref.shape[1], t_ref.shape[2], u_ref.shape[0] - 1
    t_out[...] = t_ref[...]
    u_out[...] = u_ref[...]
    t_out[0, :, :cut] = (t_ref[0, :, :cut].astype(F32) + a_ref[...].astype(F32)).astype(BF16)
    u_out[last, :, cols - cut :] = (u_ref[last, :, cols - cut :].astype(F32) + b_ref[...].astype(F32)).astype(BF16)


def close_kernel(s_ref, t_ref, u_ref, out_ref):
    n, rows = s_ref.shape[0], s_ref.shape[1] // 4
    for m in range(n):
        for z in range(4):
            at = slice(z * rows, (z + 1) * rows)
            out_ref[z, m] = (s_ref[m, at].astype(F32) + t_ref[m, at].astype(F32) + u_ref[m, at].astype(F32)).astype(BF16)


def small(kernel, args, outs, micros, limit=24, after=()):
    vmem, n_in = pl.BlockSpec(memory_space=pltpu.VMEM), len(args)

    def body(*refs):
        kernel(*refs[:n_in], *refs[n_in + len(after) :])

    return pl.pallas_call(
        body,
        in_specs=[vmem] * n_in + [pl.BlockSpec(memory_space=pl.ANY)] * len(after),
        out_specs=tuple([vmem] * len(outs)),
        out_shape=tuple(outs),
        cost_estimate=work(micros),
        compiler_params=pltpu.CompilerParams(vmem_limit_bytes=limit * MIB),
    )(*args, *after)


def several(specs, micros):
    def body(*refs):
        at, out = 0, sum(len(s[1]) for s in specs)
        for kernel, args, outs in specs:
            kernel(*refs[at : at + len(args)], *refs[out : out + len(outs)])
            at, out = at + len(args), out + len(outs)

    res = list(small(body, [a for s in specs for a in s[1]], [o for s in specs for o in s[2]], micros, 40))
    return [[res.pop(0) for _ in s[2]] for s in specs]


def flat(ref):
    k, _, r, c = ref.shape
    return ref[...].reshape(k * r, c)


def times(x, refs):
    total, at = None, 0
    for ref in refs:
        w = flat(ref)
        part = mm(x[:, at : at + w.shape[0]], w)
        total = part if total is None else total + part
        at += w.shape[0]
    return total


def times_t(x, refs, start=0, stop=None):
    return jnp.concatenate([mm_nt(x, flat(ref)[:, start:stop]) for ref in refs], axis=1)


def times_from(x, refs, start):
    total, at = None, 0
    for ref in refs:
        w = flat(ref)[:, start:]
        part = mm(x[:, at : at + w.shape[0]], w)
        total = part if total is None else total + part
        at += w.shape[0]
    return total


def split(refs, n):
    size = len(refs) // n
    return [refs[i * size : (i + 1) * size] for i in range(n)]


MIB = 1024 * 1024
SCALE = 0.2


def work(micros):
    return pl.CostEstimate(flops=int(micros * SCALE * 1.1e9), bytes_accessed=1024, transcendentals=0)


def call(kernel, args, weights, outs, cost, vmem, after=(), scratch=()):
    chunks = [c for piece in weights for c in piece]
    n_in, waits = len(args) + len(chunks), len(after)

    def body(*refs):
        kernel(*refs[:n_in], *refs[n_in + waits :])

    once = pl.Buffered(buffer_count=1)

    def whole(a):
        return pl.BlockSpec(a.shape, lambda i, nd=len(a.shape): (0,) * nd, pipeline_mode=once)

    def picked(a, m):
        k, _, r, c = a.shape
        return pl.BlockSpec((k, 1, r, c), lambda i: (0, m, 0, 0), pipeline_mode=once)

    return pl.pallas_call(
        body,
        grid=(1,),
        out_shape=tuple(outs),
        scratch_shapes=list(scratch),
        in_specs=[whole(a) for a in args] + [picked(a, m) for a, m in chunks]
        + [pl.BlockSpec(memory_space=pl.ANY)] * waits,
        out_specs=tuple(whole(o) for o in outs),
        compiler_params=pltpu.CompilerParams(vmem_limit_bytes=vmem * MIB),
        cost_estimate=cost,
    )(*args, *[a for a, m in chunks], *after)


def shape(dims, kind=F32):
    return jax.ShapeDtypeStruct(dims, kind)


def dims_of(piece):
    return [a.shape[0] * a.shape[2] for a, m in piece], piece[0][0].shape[3]


def count(w):
    return len(w), sum(len(p) for p in w)


def att_forward(x, mask, bias, vec, w, hn):
    (n, nw), (rows, width) = count(w), x.shape
    outs = [shape((rows, width)), shape((rows, width)), shape((rows, 128)), shape((n, rows, 768), BF16), shape((n, rows, 256), BF16)]
    return call(functools.partial(att_fwd_kernel, n, nw, hn), [x, mask, bias, vec], w, outs, work(4 + rows / 50), 30)


def att_backward(g, x, mask, vec, kept, w, hn, groups, after=()):
    (n, nw), (rows, width) = count(w), x.shape
    outs = [shape((rows, width)), shape((8, width)), shape((2, width))] + [shape((2 + n // groups, rows, width), BF16)] * groups
    res = call(functools.partial(att_bwd_kernel, n, nw, hn), [g, x, mask, vec] + list(kept), w, outs, work(4 + rows / 26), 30, after)
    return res[0], res[1], res[2], res[3:]


def ffn_both(x, cot, bias, vec, up, down, groups, after=()):
    (n, nw), (rows, width), f = count(up), x.shape, dims_of(up[0])[1]
    outs = [shape((rows, width)), shape((rows, width)), shape((8, width)), shape((n, f))]
    outs += [shape((2 + 2 * n // groups, rows, width), BF16)] * groups
    scratch = [pltpu.VMEM((n, rows, f), F32)]
    res = call(functools.partial(ffn_kernel, n, nw), [x, cot, bias, vec], up + down, outs, work(7 + rows / 50), 38, after, scratch)
    return res[0], res[1], res[2], res[3], res[4:]


def weight_kinds(items):
    stashes = []
    kinds = []
    for kind, arrays in items:
        at = []
        for array in arrays:
            same = [i for i, s in enumerate(stashes) if s is array]
            at.append(same[0] if same else len(stashes))
            stashes += [] if same else [array]
        kinds.append((kind, tuple(at)))
    return stashes, tuple(kinds)


def make_local(mesh):
    n_t = mesh.shape["tensor"]
    net = (Grid if (mesh.shape["dp"], n_t) == (8, 4) else Plain)(mesh)

    def local(
        lang_in, visn_in, word_len, lang_cot, visn_cot, att_in, att_out, ffn_up, ffn_down, vectors, ffn_bias1,
        att_in_m, att_in_v, att_out_m, att_out_v, ffn_up_m, ffn_up_v, ffn_down_m, ffn_down_v,
        vectors_m, vectors_v, bias1_m, bias1_v,
    ):
        width = lang_in.shape[1]
        rows = att_in.shape[1]
        cols = att_in.shape[3]
        ff = ffn_up.shape[2]
        heads_here = cols // HD
        items = word_len.shape[0]
        usable = jnp.arange(LW, dtype=jnp.int32)[None, :] < word_len[:, None]

        shards = {}
        for b in range(3):
            shards["a%d" % b] = jnp.concatenate(
                [att_in[b].astype(BF16).reshape(rows, 3 * cols), att_out[b].astype(BF16).T], axis=1
            )
        for i in range(2):
            shards["u%d" % i] = ffn_up[i].astype(BF16)
            shards["d%d" % i] = ffn_down[i].astype(BF16).T

        index_of = (net.row_blocks()[:, None] * rows + jnp.arange(rows, dtype=jnp.int32)[None, :]).reshape(-1)
        turn = (jnp.arange(width, dtype=jnp.int32)[:, None] == index_of[None, :])
        turn16, turn32 = turn.astype(BF16), turn.astype(F32)

        def to_rel(value):
            return mm(value, turn16).astype(BF16)

        def to_abs(value):
            return lax.dot_general(value, turn32, (((1,), (1,)), ((), ())), precision=HIGHEST)

        pieces = jnp.stack([net.piece_at(j) for j in range(n_t)])
        chosen = pieces[:, None] == jnp.arange(n_t, dtype=jnp.int32)[None, :]
        column = (pieces[:, None] * cols + jnp.arange(cols, dtype=jnp.int32)[None, :]).reshape(-1)
        turn_heads = (jnp.arange(width, dtype=jnp.int32)[:, None] == column[None, :]).astype(F32)

        def by_piece(value):
            return jnp.sum(jnp.where(chosen[None, :, :, None], value[:, None], 0.0), axis=2)

        vec = jnp.dot(vectors, turn32, precision=HIGHEST)
        vec_heads = jnp.dot(vectors, turn_heads, precision=HIGHEST)
        bias_ff = by_piece(ffn_bias1.reshape(2, n_t, ff))
        qv = [vec_heads[5 * b : 5 * b + 2] for b in range(3)]

        def rows3(row):
            return vec[row : row + 3]

        n_lang, n_visn = lang_in.shape[0], visn_in.shape[0]
        slots, regions = n_lang // items, n_visn // items
        item = jnp.concatenate([jnp.arange(n_lang) // slots, jnp.arange(n_visn) // regions])
        is_lang = jnp.arange(n_lang + n_visn) < n_lang
        seen = jnp.concatenate([usable.reshape(-1), jnp.ones((n_visn,), bool)])
        same = (item[:, None] == item[None, :]) & seen[None, :]
        mask0 = (same & (is_lang[:, None] != is_lang[None, :])).astype(F32)
        mask1 = same[:n_lang, :n_lang].astype(F32)
        mask2 = same[n_lang:, n_lang:].astype(F32)

        x0 = to_rel(jnp.concatenate([lang_in, visn_in], axis=0)).astype(F32)
        near, full = net.first(shards)
        later = tie({k: v for k, v in shards.items() if k != "a0"}, shards["a0"])
        pair3 = net.begin_late(("u1", "d1"), later)
        later = tie(later, near)
        pair1 = net.begin(("a1", "a2"), later, ())
        both1, *kept0 = att_forward(x0, mask0, qv[0], rows3(2), full["a0"], heads_here)
        pair3 = net.gather_late(pair3, both1)
        full.update(net.complete(pair1, both1))
        pair2 = net.begin(("u0", "d0"), later, net.begun(pair1))
        lang1, visn1 = both1[:n_lang], both1[n_lang:]
        lang2, *kept1 = att_forward(lang1, mask1, qv[1], rows3(7), full["a1"], heads_here)
        visn2, *kept2 = att_forward(visn1, mask2, qv[2], rows3(12), full["a2"], heads_here)
        full.update(net.complete(pair2, (lang2, visn2)))
        pair3 = net.complete_late(pair3, full["d0"][-1][-1][0])
        groups = net.groups
        lang_out, g_lang, sums15, bias_lang, stash = ffn_both(lang2, to_rel(lang_cot), bias_ff[0], rows3(15), full["u0"], full["d0"], groups)
        rows_f0 = net.swap_out(stash)
        g_lang, sums7, bias1, stash = att_backward(g_lang, lang1, mask1, rows3(7), kept1, full["a1"], heads_here, groups)
        rows_a1 = net.swap_out(stash)
        lang_out = to_abs(lang_out)
        part0 = net.fold_wide([("d", rows_f0), ("u", rows_f0)], [sums7, lang_out])
        full.update(net.swap_late(pair3, net.gate(part0)))
        first = ffn_both(visn2, to_rel(visn_cot), bias_ff[1], rows3(18), full["u1"], full["d1"], groups, net.gate(part0))
        visn_out, g_visn, sums18, bias_visn, stash = tie(first, net.landed(part0))
        rows_f1 = net.swap_out(stash)
        part0 = net.merge(part0, sums18)
        held0 = net.over_z(part0)
        part1 = net.send(net.fold([("d", rows_f1), ("u", rows_f1)], net.gate(part0)))
        first = att_backward(g_visn, visn1, mask2, rows3(12), kept2, full["a2"], heads_here, groups, net.gate(part1))
        (part1,) = net.bump(part1, after=first[1])
        g_visn, sums12, bias2, stash = tie(first, net.gate(part1))
        part1 = net.go(part1)
        rows_a2 = net.swap_out(stash)
        part2 = net.send(net.fold([("a", rows_a1), ("a", rows_a2)], net.gate(part1)))
        first = att_backward(
            jnp.concatenate([g_lang, g_visn], axis=0), x0, mask0, rows3(2), kept0, full["a0"], heads_here, groups, net.gate(part2)
        )
        part1, part2 = net.merge_and_bump(part1, part2, after=first[1])
        g_both, sums2, bias0, stash = tie(first, net.gate(part1))
        part2 = net.go(part2)
        rows_a0 = net.swap_out(stash)
        held1 = net.over_z(part1)
        part3 = net.send(net.fold([("a", rows_a0)], net.gate(part2)))
        blank = jnp.zeros((2, width), F32)
        by_rows = to_abs(jnp.concatenate([blank, sums2[:3], blank, sums7[:3], blank, sums12[:3], sums15[:3], sums18[:3]], axis=0))
        by_heads = lax.dot_general(
            jnp.concatenate([bias0, bias1, bias2], axis=0), turn_heads, (((1,), (1,)), ((), ())), precision=HIGHEST
        )
        lang_grad, visn_grad, visn_out = to_abs(g_both[:n_lang]), to_abs(g_both[n_lang:]), to_abs(visn_out)

        whole = []
        for b in range(3):
            whole += [by_heads[2 * b : 2 * b + 2], by_rows[5 * b + 2 : 5 * b + 5]]
        by_rows = jnp.concatenate(whole + [by_rows[15:]], axis=0)
        bias_all = by_piece(jnp.stack([bias_lang, bias_visn]))
        sums = net.first_totals(tie(jnp.concatenate([by_rows, bias_all.reshape(-1, width)], axis=0), net.gate(part3)))
        part2, part3 = net.merge_and_bump(part2, part3, after=listed(sums, held0, lang_grad, visn_grad, visn_out))
        part3 = net.go(part3)
        held2 = net.over_z(part2)
        share0, share1, share2 = net.rest(held0), net.rest(held1), net.rest(held2)

        t_in, t_in_m, t_in_v = (jnp.transpose(k, (0, 2, 1, 3)) for k in (att_in, att_in_m, att_in_v))
        up_all = (ffn_up, ffn_up_m, ffn_up_v)
        down_all = [jnp.transpose(k, (0, 2, 1)) for k in (ffn_down, ffn_down_m, ffn_down_v)]
        ffn_new = adam_call(adam_ffn_kernel, (0,), share0[1::-1], [up_all, down_all], None)
        ffn_new = adam_call(adam_ffn_kernel, (1,), share1[1::-1], [up_all, down_all], ffn_new)
        sums = net.next_total(sums, "x", net.gate(part2))
        part3 = net.merge(part3, [ffn_new[0], sums])
        sums = net.next_total(sums, "y", net.gate(part3))
        vector_grad, bias1_grad = sums[:21], sums[21:].reshape(ffn_bias1.shape)

        att_all = [(t_in, t_in_m, t_in_v), (att_out, att_out_m, att_out_v)]
        att_new = adam_call(adam_att_kernel, (1,), share2[:1], att_all, None)
        att_new = adam_call(adam_att_kernel, (2,), share2[1:], att_all, att_new)
        share3 = net.rest(net.over_z(part3, att_new[0]))
        att_new = adam_call(adam_att_kernel, (0,), share3, att_all, att_new)
        in_new = [jnp.transpose(k, (0, 2, 1, 3)) for k in att_new[:5]]

        result = [lang_out, visn_out, lang_grad, visn_grad] + in_new + list(att_new[5:]) + list(ffn_new[:5]) + [jnp.transpose(k, (0, 2, 1)) for k in ffn_new[5:]]
        for share, weight, first, second, rate in (
            (vector_grad, vectors, vectors_m, vectors_v, rate_vector),
            (bias1_grad, ffn_bias1, bias1_m, bias1_v, rate_bias),
        ):
            m_new, v_new, w_new = adam_step(weight, share, first, second, rate)
            result += [share, m_new, v_new, w_new]
        return tuple(result)

    return local


def solution(mesh):
    rows = P(("dp", "tensor"), None)
    w_in, w_out, w_up, w_down = P(None, "dp", None, "tensor"), P(None, "tensor", "dp"), P(None, "dp", "tensor"), P(None, "tensor", "dp")
    return jax.shard_map(
        make_local(mesh),
        mesh=mesh,
        in_specs=(rows, rows, P(("dp", "tensor")), rows, rows, w_in, w_out, w_up, w_down, P(), P())
        + (w_in,) * 2 + (w_out,) * 2 + (w_up,) * 2 + (w_down,) * 2 + (P(),) * 4,
        out_specs=(rows,) * 4 + (w_in,) * 5 + (w_out,) * 5 + (w_up,) * 5 + (w_down,) * 5 + (P(),) * 8,
        check_vma=False,
    )
```

profile of v0, /device:TPU:0, one launch (start us, length us, event | category | flops | bytes accessed | tf_op | source)
XLA Modules:
  0.0 385.9 jit_solution(9750940341967941884)
XLA Ops:
  10.8 5.0 %collective-permute-start.2 = (bf16[1,96,768]{2,1,0:T(8,128)(2,1)}, bf16[1,96,768]{2,1,0:T(8,128)(2,1)S(1)}, u32[]{:S(2)}, u32[]{:S(2)}) collective-permute-start(bf16[1,96,768]{2,1,0:T(8,128)(2,1)} %bitcast.18), channel_id=1, source_target_pairs={{0,24},{4,28},{8,16},{12,20},{16,8},{20,12},{24,0},{28,4},{1,25},{... | collective-permute-start | bytes 442376 | tf_op jit(solution)/shard_map/ppermute | solution.py:142
  21.4 4.3 %collective-permute-done = bf16[1,96,768]{2,1,0:T(8,128)(2,1)} collective-permute-done((bf16[1,96,768]{2,1,0:T(8,128)(2,1)}, bf16[1,96,768]{2,1,0:T(8,128)(2,1)}, u32[]{:S(2)}, u32[]{:S(2)}) %collective-permute-start) | collective-permute-done | bytes 147488 | tf_op jit(solution)/shard_map/ppermute | solution.py:142
  36.0 8.5 %collective-permute-done.6.refs_8_.refs_12_ = bf16[4,1,96,768]{3,2,1,0:T(8,128)(2,1)} collective-permute-done((bf16[4,1,96,768]{3,2,1,0:T(8,128)(2,1)S(1)}, bf16[4,1,96,768]{3,2,1,0:T(8,128)(2,1)}, u32[]{:S(2)}, u32[]{:S(2)}) %collective-permute-start.6) | collective-permute-done | bytes 589856 | tf_op jit(solution)/shard_map/ppermute | solution.py:142
  50.7 6.8 %all-gather.7.cloned.1.call-done = bf16[8,96,768]{2,1,0:T(8,128)(2,1)} async-done(((bf16[2,96,768]{2,1,0:T(8,128)(2,1)}), bf16[8,96,768]{2,1,0:T(8,128)(2,1)}) %all-gather.7.cloned.1.call-update) | async-done | bytes 1179664 | tf_op jit(solution)/shard_map/all_gather | solution.py:181
  65.8 2.7 fusion.12.refs_0_.refs_1_
  73.2 11.8 %shard_map.470 = (f32[336,768]{1,0:T(8,128)S(1)}, f32[336,768]{1,0:T(8,128)S(1)}, f32[336,128]{1,0:T(8,128)S(1)}, bf16[4,336,768]{2,1,0:T(8,128)(2,1)S(1)}, bf16[4,336,256]{2,1,0:T(8,128)(2,1)S(1)}) custom-call(f32[336,768]{1,0:T(8,128)S(1)} %copy-done.107, f32[336,336]{1,0:T(8,128)S(1)} %copy-done.64, f32[2,768]{1,0:T(2,128)S(1)} %get-tuple-element.435.refs_2_, ...), custom_call_target="tpu_custom_call" | custom-call | flops 2358400000 | bytes 1024 | tf_op jit(solution)/shard_map/pallas_call | solution.py:663
  92.0 12.8 %collective-permute-done.15.refs_9_.refs_13_ = bf16[4,1,96,768]{3,2,1,0:T(8,128)(2,1)S(1)} collective-permute-done((bf16[4,1,96,768]{3,2,1,0:T(8,128)(2,1)S(1)}, bf16[4,1,96,768]{3,2,1,0:T(8,128)(2,1)S(1)}, u32[]{:S(2)}, u32[]{:S(2)}) %collective-permute-start.15) | collective-permute-done | bytes 589856 | tf_op jit(solution)/shard_map/ppermute | solution.py:142
  111.4 6.5 %shard_map.471 = (f32[120,768]{1,0:T(8,128)S(1)}, f32[120,768]{1,0:T(8,128)S(1)}, f32[120,128]{1,0:T(8,128)S(1)}, bf16[4,120,768]{2,1,0:T(8,128)(2,1)S(1)}, bf16[4,120,256]{2,1,0:T(8,128)(2,1)S(1)}) custom-call(f32[120,768]{1,0:T(8,128)S(1)} %slice.194.refs_0_.refs_1_, f32[120,120]{1,0:T(8,128)S(1)} %slice_convert_fusion.1.refs_1_.refs_2_, ...), custom_call_target="tpu_custom_call" | custom-call | flops 1408000000 | bytes 1024 | tf_op jit(solution)/shard_map/pallas_call | solution.py:663
  121.6 7.6 %shard_map.472 = (f32[216,768]{1,0:T(8,128)S(1)}, f32[216,768]{1,0:T(8,128)S(1)}, f32[216,128]{1,0:T(8,128)S(1)}, bf16[4,216,768]{2,1,0:T(8,128)(2,1)S(1)}, bf16[4,216,256]{2,1,0:T(8,128)(2,1)S(1)}) custom-call(f32[216,768]{1,0:T(8,128)S(1)} %slice.209.refs_0_.refs_1_, f32[216,216]{1,0:T(8,128)S(1)} %slice_convert_fusion.refs_1_.refs_2_, ...), custom_call_target="tpu_custom_call" | custom-call | flops 1830400000 | bytes 1024 | tf_op jit(solution)/shard_map/pallas_call | solution.py:663
  130.8 3.5 collective-permute-done.21.refs_8_.refs_16_
  140.3 10.3 %collective-permute-done.27.refs_17_ = bf16[4,1,96,768]{3,2,1,0:T(8,128)(2,1)} collective-permute-done((bf16[4,1,96,768]{3,2,1,0:T(8,128)(2,1)S(1)}, bf16[4,1,96,768]{3,2,1,0:T(8,128)(2,1)}, u32[]{:S(2)}, u32[]{:S(2)}) %collective-permute-start.27) | collective-permute-done | bytes 589856 | tf_op jit(solution)/shard_map/ppermute | solution.py:142
  156.9 3.3 fusion.52
  162.5 10.3 %shard_map.473 = (f32[120,768]{1,0:T(8,128)S(1)}, f32[120,768]{1,0:T(8,128)S(1)}, f32[8,768]{1,0:T(8,128)S(1)}, f32[4,768]{1,0:T(4,128)S(1)}, bf16[6,120,768]{2,...) custom-call(f32[120,768]{1,0:T(8,128)S(1)} %copy-done.74, bf16[120,768]{1,0:T(8,128)(2,1)S(1)} %copy-done.77, ...), custom_call_target="tpu_custom_call" | custom-call | flops 2068000000 | bytes 1024 | tf_op jit(solution)/shard_map/pallas_call | solution.py:663
  173.0 7.1 %shard_map.474 = (f32[120,768]{1,0:T(8,128)S(1)}, f32[8,768]{1,0:T(8,128)S(1)}, f32[2,768]{1,0:T(2,128)S(1)}, bf16[4,120,768]{2,1,0:T(8,128)(2,1)S(1)}, bf16[4,120,768]{2,1,0:T(8,128)(2,1)S(1)}) custom-call(f32[120,768]{1,0:T(8,128)S(1)} %get-tuple-element.235.refs_0_, f32[120,768]{1,0:T(8,128)S(1)} %copy-done.19, ...), custom_call_target="tpu_custom_call" | custom-call | flops 1895384576 | bytes 1024 | tf_op jit(solution)/shard_map/pallas_call | solution.py:663
  181.6 2.6 shard_map.475
  185.8 2.9 collective-permute-done.33.refs_16_.refs_17_
  194.3 9.6 %shard_map.476 = (f32[216,768]{1,0:T(8,128)S(1)}, f32[216,768]{1,0:T(8,128)S(1)}, f32[8,768]{1,0:T(8,128)S(1)}, f32[4,768]{1,0:T(4,128)S(1)}, bf16[6,216,768]{2,...) custom-call(f32[216,768]{1,0:T(8,128)S(1)} %copy-done.53, bf16[216,768]{1,0:T(8,128)(2,1)S(1)} %fusion.14.refs_1_, ...), custom_call_target="tpu_custom_call" | custom-call | flops 2490400000 | bytes 1024 | tf_op jit(solution)/shard_map/pallas_call | solution.py:663
  206.9 11.2 %collective-permute-done.37.refs_1_ = bf16[2,384,768]{2,1,0:T(8,128)(2,1)S(1)} collective-permute-done((bf16[2,384,768]{2,1,0:T(8,128)(2,1)S(1)}, bf16[2,384,768]{2,1,0:T(8,128)(2,1)S(1)}, u32[]{:S(2)}, u32[]{:S(2)}) %collective-permute-start.37) | collective-permute-done | bytes 1179680 | tf_op jit(solution)/shard_map/ppermute | solution.py:142
  220.5 2.4 collective-permute-done.39.refs_1_
  226.3 4.4 %shard_map.478 = (bf16[2,384,768]{2,1,0:T(8,128)(2,1)S(1)}, bf16[2,384,768]{2,1,0:T(8,128)(2,1)S(1)}, bf16[2,384,768]{2,1,0:T(8,128)(2,1)S(1)}, bf16[384,768]{1,0:T(8,128)(2,1)S(1)}, bf16[384,768]{1,0:T(8,128)(2,1)S(1)}) custom-call(bf16[6,216,768]{2,1,0:T(8,128)(2,1)S(1)} %copy-done.38, bf16[6,216,768]{2,1,0:T(8,128)(2,1)} %collective-permute-done.39.refs_1_, ...), custom_call_target="tpu_custom_call" | custom-call | flops 660000000 | bytes 1024 | tf_op jit(solution)/shard_map/pallas_call | solution.py:584
  232.8 9.0 %shard_map.479 = (f32[216,768]{1,0:T(8,128)S(1)}, f32[8,768]{1,0:T(8,128)S(1)}, f32[2,768]{1,0:T(2,128)S(1)}, bf16[4,216,768]{2,1,0:T(8,128)(2,1)S(1)}, bf16[4,216,768]{2,1,0:T(8,128)(2,1)S(1)}) custom-call(f32[216,768]{1,0:T(8,128)S(1)} %copy-done.57, f32[216,768]{1,0:T(8,128)S(1)} %slice.209.refs_0_.refs_1_, f32[216,216]{1,0:T(8,128)S(1)} %copy-done.36, ...), custom_call_target="tpu_custom_call" | custom-call | flops 2707692288 | bytes 1024 | tf_op jit(solution)/shard_map/pallas_call | solution.py:663
  241.7 4.5 %collective-permute-done.40.refs_2_ = bf16[384,768]{1,0:T(8,128)(2,1)S(1)} collective-permute-done((bf16[384,768]{1,0:T(8,128)(2,1)S(1)}, bf16[384,768]{1,0:T(8,128)(2,1)S(1)}, u32[]{:S(2)}, u32[]{:S(2)}) %collective-permute-start.40) | collective-permute-done | bytes 589856 | tf_op jit(solution)/shard_map/ppermute | solution.py:142
  250.9 4.0 %shard_map.481 = (bf16[2,384,768]{2,1,0:T(8,128)(2,1)S(1)}, bf16[2,384,768]{2,1,0:T(8,128)(2,1)S(1)}, bf16[2,384,768]{2,1,0:T(8,128)(2,1)S(1)}, bf16[384,768]{1,0:T(8,128)(2,1)S(1)}, bf16[384,768]{1,0:T(8,128)(2,1)S(1)}) custom-call(bf16[4,120,768]{2,1,0:T(8,128)(2,1)S(1)} %copy-done.49, bf16[4,120,768]{2,1,0:T(8,128)(2,1)S(1)} %collective-permute-done.42.refs_1_, ...), custom_call_target="tpu_custom_call" | custom-call | flops 660000000 | bytes 1024 | tf_op jit(solution)/shard_map/pallas_call | solution.py:584
  258.3 15.9 %shard_map.482 = (f32[336,768]{1,0:T(8,128)S(1)}, f32[8,768]{1,0:T(8,128)S(1)}, f32[2,768]{1,0:T(2,128)S(1)}, bf16[4,336,768]{2,1,0:T(8,128)(2,1)S(1)}, bf16[4,336,768]{2,1,0:T(8,128)(2,1)S(1)}) custom-call(f32[336,768]{1,0:T(8,128)S(1)} %pad_maximum_fusion.refs_0_, f32[336,768]{1,0:T(8,128)S(1)} %copy-done.108, f32[336,336]{1,0:T(8,128)S(1)} %copy-done.65, ...), custom_call_target="tpu_custom_call" | custom-call | flops 3723076864 | bytes 1024 | tf_op jit(solution)/shard_map/pallas_call | solution.py:663
  277.6 11.5 %collective-permute-done.46.refs_5_ = bf16[384,768]{1,0:T(8,128)(2,1)S(1)} collective-permute-done((bf16[384,768]{1,0:T(8,128)(2,1)S(1)}, bf16[384,768]{1,0:T(8,128)(2,1)S(1)}, u32[]{:S(2)}, u32[]{:S(2)}) %collective-permute-start.46) | collective-permute-done | bytes 589856 | tf_op jit(solution)/shard_map/ppermute | solution.py:142
  300.5 5.1 %shard_map.484 = (bf16[1,384,768]{2,1,0:T(8,128)(2,1)S(1)}, bf16[1,384,768]{2,1,0:T(8,128)(2,1)S(1)}, bf16[1,384,768]{2,1,0:T(8,128)(2,1)S(1)}, bf16[384,384]{1,0:T(8,128)(2,1)}, bf16[384,384]{1,0:T(8,128)(2,1)S(1)}) custom-call(bf16[4,336,768]{2,1,0:T(8,128)(2,1)S(1)} %get-tuple-element.306.refs_0_, bf16[4,336,768]{2,1,0:T(8,128)(2,1)} %collective-permute-done.48.refs_1_, ...), custom_call_target="tpu_custom_call" | custom-call | flops 660000000 | bytes 1024 | tf_op jit(solution)/shard_map/pallas_call | solution.py:584
  313.4 5.8 %collective-permute-done.52 = f32[29,768]{1,0:T(8,128)S(1)} collective-permute-done((f32[29,768]{1,0:T(8,128)S(1)}, f32[29,768]{1,0:T(8,128)S(1)}, u32[]{:S(2)}, u32[]{:S(2)}) %collective-permute-start.52) | collective-permute-done | bytes 89120 | tf_op jit(solution)/shard_map/ppermute | solution.py:142
  321.6 5.1 %collective-permute-done.53 = f32[29,768]{1,0:T(8,128)S(1)} collective-permute-done((f32[29,768]{1,0:T(8,128)S(1)}, f32[29,768]{1,0:T(8,128)S(1)}, u32[]{:S(2)}, u32[]{:S(2)}) %collective-permute-start.53) | collective-permute-done | bytes 89120 | tf_op jit(solution)/shard_map/ppermute | solution.py:142
  326.7 3.4 collective-permute-done.56.refs_5_
  331.2 2.4 shard_map.487
  343.3 2.5 collective-permute-done.49
  353.9 3.4 collective-permute-done.58
  (481 shorter events, 163.7 us)
Async XLA Ops:
  7.2 50.2 %all-gather.7.cloned.1.call-start = ((), (), s32[]{:S(2)}) async-start(), calls=%async_computation.6 | async-start | bytes 1474560 | tf_op jit(solution)/shard_map/all_gather | solution.py:181
  17.9 45.9 %collective-permute-start.30 = (bf16[96,768]{1,0:T(8,128)(2,1)S(1)}, bf16[96,768]{1,0:T(8,128)(2,1)}, u32[]{:S(2)}, u32[]{:S(2)}) collective-permute-start(bf16[96,768]{1,0:T(8,128)(2,1)S(1)} %get-tuple-element.216), channel_id=1, source_target_pairs={{0,4},{4,0},{8,12},{12,8},{16,20},{20,16},{24,28},{28,24},{1,5},{5... | collective-permute-start | bytes 442376 | tf_op jit(solution)/shard_map/ppermute | solution.py:142
  19.7 44.1 %collective-permute-start.29 = (bf16[96,768]{1,0:T(8,128)(2,1)}, bf16[96,768]{1,0:T(8,128)(2,1)}, u32[]{:S(2)}, u32[]{:S(2)}) collective-permute-start(bf16[96,768]{1,0:T(8,128)(2,1)} %get-tuple-element.218), channel_id=1, source_target_pairs={{0,2},{1,3},{2,0},{3,1},{4,6},{5,7},{6,4},{7,5},{8,10},{9,11},{10,... | collective-permute-start | bytes 442376 | tf_op jit(solution)/shard_map/ppermute | solution.py:142
  26.7 78.9 %all-gather.9.cloned.1.call-start = ((), (), s32[]{:S(2)}) async-start(), calls=%async_computation.7 | async-start | bytes 1474560 | tf_op jit(solution)/shard_map/all_gather | solution.py:181
  33.9 122.9 %all-gather.11.cloned.1.call-start = ((), (), s32[]{:S(2)}) async-start(), calls=%async_computation.8 | async-start | bytes 2949120 | tf_op jit(solution)/shard_map/all_gather | solution.py:192
  36.0 28.4 %collective-permute-start.4 = (bf16[4,1,96,768]{3,2,1,0:T(8,128)(2,1)S(1)}, bf16[4,1,96,768]{3,2,1,0:T(8,128)(2,1)}, u32[]{:S(2)}, u32[]{:S(2)}) collective-permute-start(bf16[4,1,96,768]{3,2,1,0:T(8,128)(2,1)S(1)} %bitcast_dynamic-update-slice_fusion.refs_4_.refs_8_), channel_id=1, source_target_pairs={{0,1},{1,0},{2,3},{3,2},{4,5},{5,4},{6,7},{7,6},{8,9},{9,8},{10,11... | collective-permute-start | bytes 1769480 | tf_op jit(solution)/shard_map/ppermute | solution.py:142
  57.5 31.9 %collective-permute-start.14 = (bf16[4,2,96,768]{3,2,1,0:T(8,128)(2,1)}, bf16[4,2,96,768]{3,2,1,0:T(8,128)(2,1)S(1)}, u32[]{:S(2)}, u32[]{:S(2)}) collective-permute-start(bf16[4,2,96,768]{3,2,1,0:T(8,128)(2,1)} %bitcast.134), channel_id=1, source_target_pairs={{0,2},{1,3},{2,0},{3,1},{4,6},{5,7},{6,4},{7,5},{8,10},{9,11},{10,... | collective-permute-start | bytes 3538952 | tf_op jit(solution)/shard_map/ppermute | solution.py:142
  58.9 30.5 %collective-permute-start.11 = (bf16[4,2,96,768]{3,2,1,0:T(8,128)(2,1)}, bf16[4,2,96,768]{3,2,1,0:T(8,128)(2,1)S(1)}, u32[]{:S(2)}, u32[]{:S(2)}) collective-permute-start(bf16[4,2,96,768]{3,2,1,0:T(8,128)(2,1)} %bitcast.135), channel_id=1, source_target_pairs={{0,4},{4,0},{8,12},{12,8},{16,20},{20,16},{24,28},{28,24},{1,5},{5... | collective-permute-start | bytes 3538952 | tf_op jit(solution)/shard_map/ppermute | solution.py:142
  70.5 35.1 %collective-permute-start.12 = (bf16[4,2,96,768]{3,2,1,0:T(8,128)(2,1)}, bf16[4,2,96,768]{3,2,1,0:T(8,128)(2,1)}, u32[]{:S(2)}, u32[]{:S(2)}) collective-permute-start(bf16[4,2,96,768]{3,2,1,0:T(8,128)(2,1)} %bitcast.136), channel_id=1, source_target_pairs={{0,1},{1,0},{2,3},{3,2},{4,5},{5,4},{6,7},{7,6},{8,9},{9,8},{10,11... | collective-permute-start | bytes 3538952 | tf_op jit(solution)/shard_map/ppermute | solution.py:142
  89.2 237.5 %reduce-scatter.6.cloned.1.call-start = ((), (), s32[]{:S(2)}) async-start(), calls=%async_computation.4 | async-start | bytes 2949120 | tf_op jit(solution)/shard_map/reduce_scatter | solution.py:284
  91.5 19.9 %collective-permute-start.16 = (bf16[4,2,96,768]{3,2,1,0:T(8,128)(2,1)S(1)}, bf16[4,2,96,768]{3,2,1,0:T(8,128)(2,1)}, u32[]{:S(2)}, u32[]{:S(2)}) collective-permute-start(bf16[4,2,96,768]{3,2,1,0:T(8,128)(2,1)S(1)} %collective-permute-done.14.refs_8_.refs_12_), channel_id=1, source_target_pairs={{0,1},{1,0},{2,3},{3,2},{4,5},{5,4},{6,7},{7,6},{8,9},{9,8},{10,11... | collective-permute-start | bytes 3538952 | tf_op jit(solution)/shard_map/ppermute | solution.py:142
  91.5 19.9 %collective-permute-start.13 = (bf16[4,2,96,768]{3,2,1,0:T(8,128)(2,1)S(1)}, bf16[4,2,96,768]{3,2,1,0:T(8,128)(2,1)}, u32[]{:S(2)}, u32[]{:S(2)}) collective-permute-start(bf16[4,2,96,768]{3,2,1,0:T(8,128)(2,1)S(1)} %collective-permute-done.11.refs_5_.refs_9_), channel_id=1, source_target_pairs={{0,1},{1,0},{2,3},{3,2},{4,5},{5,4},{6,7},{7,6},{8,9},{9,8},{10,11... | collective-permute-start | bytes 3538952 | tf_op jit(solution)/shard_map/ppermute | solution.py:142
  105.6 28.7 %collective-permute-start.21 = (bf16[4,2,96,768]{3,2,1,0:T(8,128)(2,1)}, bf16[4,2,96,768]{3,2,1,0:T(8,128)(2,1)}, u32[]{:S(2)}, u32[]{:S(2)}) collective-permute-start(bf16[4,2,96,768]{3,2,1,0:T(8,128)(2,1)} %bitcast.41.refs_4_.refs_12_), channel_id=1, source_target_pairs={{0,2},{1,3},{2,0},{3,1},{4,6},{5,7},{6,4},{7,5},{8,10},{9,11},{10,... | collective-permute-start | bytes 3538952 | tf_op jit(solution)/shard_map/ppermute | solution.py:142
  106.3 28.3 %collective-permute-start.18 = (bf16[4,2,96,768]{3,2,1,0:T(8,128)(2,1)}, bf16[4,2,96,768]{3,2,1,0:T(8,128)(2,1)}, u32[]{:S(2)}, u32[]{:S(2)}) collective-permute-start(bf16[4,2,96,768]{3,2,1,0:T(8,128)(2,1)} %bitcast.41.refs_4_.refs_12_), channel_id=1, source_target_pairs={{0,4},{4,0},{8,12},{12,8},{16,20},{20,16},{24,28},{28,24},{1,5},{5... | collective-permute-start | bytes 3538952 | tf_op jit(solution)/shard_map/ppermute | solution.py:142
  139.8 20.5 %collective-permute-start.19 = (bf16[4,2,96,768]{3,2,1,0:T(8,128)(2,1)}, bf16[4,2,96,768]{3,2,1,0:T(8,128)(2,1)}, u32[]{:S(2)}, u32[]{:S(2)}) collective-permute-start(bf16[4,2,96,768]{3,2,1,0:T(8,128)(2,1)} %bitcast.41.refs_4_.refs_12_), channel_id=1, source_target_pairs={{0,1},{1,0},{2,3},{3,2},{4,5},{5,4},{6,7},{7,6},{8,9},{9,8},{10,11... | collective-permute-start | bytes 3538952 | tf_op jit(solution)/shard_map/ppermute | solution.py:142
  139.8 22.6 %collective-permute-start.25 = (bf16[4,2,96,768]{3,2,1,0:T(8,128)(2,1)}, bf16[4,2,96,768]{3,2,1,0:T(8,128)(2,1)}, u32[]{:S(2)}, u32[]{:S(2)}) collective-permute-start(bf16[4,2,96,768]{3,2,1,0:T(8,128)(2,1)} %collective-permute-done.21.refs_8_.refs_16_), channel_id=1, source_target_pairs={{0,1},{1,0},{2,3},{3,2},{4,5},{5,4},{6,7},{7,6},{8,9},{9,8},{10,11... | collective-permute-start | bytes 3538952 | tf_op jit(solution)/shard_map/ppermute | solution.py:142
  140.3 22.1 %collective-permute-start.20 = (bf16[4,2,96,768]{3,2,1,0:T(8,128)(2,1)}, bf16[4,2,96,768]{3,2,1,0:T(8,128)(2,1)}, u32[]{:S(2)}, u32[]{:S(2)}) collective-permute-start(bf16[4,2,96,768]{3,2,1,0:T(8,128)(2,1)} %collective-permute-done.18.refs_5_.refs_13_), channel_id=1, source_target_pairs={{0,1},{1,0},{2,3},{3,2},{4,5},{5,4},{6,7},{7,6},{8,9},{9,8},{10,11... | collective-permute-start | bytes 3538952 | tf_op jit(solution)/shard_map/ppermute | solution.py:142
  156.8 35.3 %collective-permute-start.32 = (bf16[4,4,96,768]{3,2,1,0:T(8,128)(2,1)}, bf16[4,4,96,768]{3,2,1,0:T(8,128)(2,1)S(1)}, u32[]{:S(2)}, u32[]{:S(2)}) collective-permute-start(bf16[4,4,96,768]{3,2,1,0:T(8,128)(2,1)} %bitcast.128), channel_id=1, source_target_pairs={{0,1},{1,0},{2,3},{3,2},{4,5},{5,4},{6,7},{7,6},{8,9},{9,8},{10,11... | collective-permute-start | bytes 7077896 | tf_op jit(solution)/shard_map/ppermute | solution.py:142
  160.2 28.5 %collective-permute-start.33 = (bf16[4,2,96,768]{3,2,1,0:T(8,128)(2,1)}, bf16[4,2,96,768]{3,2,1,0:T(8,128)(2,1)S(1)}, u32[]{:S(2)}, u32[]{:S(2)}) collective-permute-start(bf16[4,2,96,768]{3,2,1,0:T(8,128)(2,1)} %get-tuple-element.403), channel_id=1, source_target_pairs={{0,2},{1,3},{2,0},{3,1},{4,6},{5,7},{6,4},{7,5},{8,10},{9,11},{10,... | collective-permute-start | bytes 3538952 | tf_op jit(solution)/shard_map/ppermute | solution.py:142
  161.6 28.2 %collective-permute-start.31 = (bf16[4,2,96,768]{3,2,1,0:T(8,128)(2,1)}, bf16[4,2,96,768]{3,2,1,0:T(8,128)(2,1)S(1)}, u32[]{:S(2)}, u32[]{:S(2)}) collective-permute-start(bf16[4,2,96,768]{3,2,1,0:T(8,128)(2,1)} %get-tuple-element.404), channel_id=1, source_target_pairs={{0,4},{4,0},{8,12},{12,8},{16,20},{20,16},{24,28},{28,24},{1,5},{5... | collective-permute-start | bytes 3538952 | tf_op jit(solution)/shard_map/ppermute | solution.py:142
  190.3 27.9 %collective-permute-start.37 = (bf16[2,384,768]{2,1,0:T(8,128)(2,1)S(1)}, bf16[2,384,768]{2,1,0:T(8,128)(2,1)S(1)}, u32[]{:S(2)}, u32[]{:S(2)}) collective-permute-start(bf16[2,384,768]{2,1,0:T(8,128)(2,1)S(1)} %get-tuple-element.250), channel_id=1, source_target_pairs={{0,4},{4,0},{8,12},{12,8},{16,20},{20,16},{24,28},{28,24},{1,5},{5... | collective-permute-start | bytes 3538952 | tf_op jit(solution)/shard_map/ppermute | solution.py:142
  190.9 27.6 %collective-permute-start.38 = (bf16[2,384,768]{2,1,0:T(8,128)(2,1)S(1)}, bf16[2,384,768]{2,1,0:T(8,128)(2,1)S(1)}, u32[]{:S(2)}, u32[]{:S(2)}) collective-permute-start(bf16[2,384,768]{2,1,0:T(8,128)(2,1)S(1)} %get-tuple-element.251), channel_id=1, source_target_pairs={{0,2},{1,3},{2,0},{3,1},{4,6},{5,7},{6,4},{7,5},{8,10},{9,11},{10,... | collective-permute-start | bytes 3538952 | tf_op jit(solution)/shard_map/ppermute | solution.py:142
  220.4 129.7 %reduce-scatter.4.cloned.1.call-start = ((), (), s32[]{:S(2)}) async-start(), calls=%async_computation.3 | async-start | bytes 1474560 | tf_op jit(solution)/shard_map/reduce_scatter | solution.py:284
  247.3 29.3 %collective-permute-start.44 = (bf16[2,384,768]{2,1,0:T(8,128)(2,1)S(1)}, bf16[2,384,768]{2,1,0:T(8,128)(2,1)S(1)}, u32[]{:S(2)}, u32[]{:S(2)}) collective-permute-start(bf16[2,384,768]{2,1,0:T(8,128)(2,1)S(1)} %get-tuple-element.277.refs_4_), channel_id=1, source_target_pairs={{0,4},{4,0},{8,12},{12,8},{16,20},{20,16},{24,28},{28,24},{1,5},{5... | collective-permute-start | bytes 3538952 | tf_op jit(solution)/shard_map/ppermute | solution.py:142
  248.7 28.9 %collective-permute-start.45 = (bf16[2,384,768]{2,1,0:T(8,128)(2,1)S(1)}, bf16[2,384,768]{2,1,0:T(8,128)(2,1)S(1)}, u32[]{:S(2)}, u32[]{:S(2)}) collective-permute-start(bf16[2,384,768]{2,1,0:T(8,128)(2,1)S(1)} %get-tuple-element.295), channel_id=1, source_target_pairs={{0,2},{1,3},{2,0},{3,1},{4,6},{5,7},{6,4},{7,5},{8,10},{9,11},{10,... | collective-permute-start | bytes 3538952 | tf_op jit(solution)/shard_map/ppermute | solution.py:142
  255.0 34.1 %collective-permute-start.46 = (bf16[384,768]{1,0:T(8,128)(2,1)S(1)}, bf16[384,768]{1,0:T(8,128)(2,1)S(1)}, u32[]{:S(2)}, u32[]{:S(2)}) collective-permute-start(bf16[384,768]{1,0:T(8,128)(2,1)S(1)} %get-tuple-element.302), channel_id=1, source_target_pairs={{0,2},{1,3},{2,0},{3,1},{4,6},{5,7},{6,4},{7,5},{8,10},{9,11},{10,... | collective-permute-start | bytes 1769480 | tf_op jit(solution)/shard_map/ppermute | solution.py:142
  256.6 32.4 %collective-permute-start.47 = (bf16[384,768]{1,0:T(8,128)(2,1)S(1)}, bf16[384,768]{1,0:T(8,128)(2,1)S(1)}, u32[]{:S(2)}, u32[]{:S(2)}) collective-permute-start(bf16[384,768]{1,0:T(8,128)(2,1)S(1)} %get-tuple-element.303), channel_id=1, source_target_pairs={{0,4},{4,0},{8,12},{12,8},{16,20},{20,16},{24,28},{28,24},{1,5},{5... | collective-permute-start | bytes 1769480 | tf_op jit(solution)/shard_map/ppermute | solution.py:142
  293.0 76.5 %reduce-scatter.8.cloned.1.call-start = ((), (), s32[]{:S(2)}) async-start(), calls=%async_computation.5 | async-start | bytes 1474560 | tf_op jit(solution)/shard_map/reduce_scatter | solution.py:284
  295.3 31.4 %collective-permute-start.54 = (bf16[2,384,768]{2,1,0:T(8,128)(2,1)}, bf16[2,384,768]{2,1,0:T(8,128)(2,1)}, u32[]{:S(2)}, u32[]{:S(2)}) collective-permute-start(bf16[2,384,768]{2,1,0:T(8,128)(2,1)} %copy-done.45), channel_id=1, source_target_pairs={{0,4},{4,0},{8,12},{12,8},{16,20},{20,16},{24,28},{28,24},{1,5},{5... | collective-permute-start | bytes 3538952 | tf_op jit(solution)/shard_map/ppermute | solution.py:142
  296.0 30.7 %collective-permute-start.55 = (bf16[2,384,768]{2,1,0:T(8,128)(2,1)}, bf16[2,384,768]{2,1,0:T(8,128)(2,1)}, u32[]{:S(2)}, u32[]{:S(2)}) collective-permute-start(bf16[2,384,768]{2,1,0:T(8,128)(2,1)} %copy-done.94), channel_id=1, source_target_pairs={{0,2},{1,3},{2,0},{3,1},{4,6},{5,7},{6,4},{7,5},{8,10},{9,11},{10,... | collective-permute-start | bytes 3538952 | tf_op jit(solution)/shard_map/ppermute | solution.py:142
  308.0 22.1 %collective-permute-start.56 = (bf16[384,384]{1,0:T(8,128)(2,1)}, bf16[384,384]{1,0:T(8,128)(2,1)S(1)}, u32[]{:S(2)}, u32[]{:S(2)}) collective-permute-start(bf16[384,384]{1,0:T(8,128)(2,1)} %get-tuple-element.340), channel_id=1, source_target_pairs={{0,2},{1,3},{2,0},{3,1},{4,6},{5,7},{6,4},{7,5},{8,10},{9,11},{10,... | collective-permute-start | bytes 884744 | tf_op jit(solution)/shard_map/ppermute | solution.py:142
  308.4 21.7 %collective-permute-start.57 = (bf16[384,384]{1,0:T(8,128)(2,1)S(1)}, bf16[384,384]{1,0:T(8,128)(2,1)S(1)}, u32[]{:S(2)}, u32[]{:S(2)}) collective-permute-start(bf16[384,384]{1,0:T(8,128)(2,1)S(1)} %get-tuple-element.341), channel_id=1, source_target_pairs={{0,4},{4,0},{8,12},{12,8},{16,20},{20,16},{24,28},{28,24},{1,5},{5... | collective-permute-start | bytes 884744 | tf_op jit(solution)/shard_map/ppermute | solution.py:142
  (161 other events, 1345.2 us)
Sparse Core Ops, SparseCore 0:
  26.9 30.5 all-gather.6
  59.6 29.5 all-gather.8
  91.3 49.5 all-gather.10
  220.5 46.5 reduce-scatter.5
  293.1 30.1 reduce-scatter.3
  336.3 28.6 reduce-scatter.7
where the time goes:
time: 390 us; the launch traced here: 386 us
  waiting for transfers between devices  108 us (28%)
  Pallas kernels  107 us (27%)
  local copies, waits for them, and re-layouts  65.4 us (17%)
  starting transfers between devices  55.3 us (14%)
  matrix products  18 us (5%)
  between operations  16 us (4%)
  other arithmetic  15.7 us (4%)
    ppermute x65, waiting for transfers between devices, swap(): return lax.ppermute(value, axis, [(i, i ^ mask) for i in range(size)])  101 us
    pallas_call x8, Pallas kernels, call(): pl.pallas_call(body, grid=(1,), out_shape=tuple(outs), scratch_shapes=lis...  77.8 us
    ppermute x65, starting transfers between devices, swap(): return lax.ppermute(value, axis, [(i, i ^ mask) for i in range(size)])  54.4 us
    unnamed x246, local copies, waits for them, and re-layouts  38.9 us
    pallas_call x9, Pallas kernels, small(): pl.pallas_call(body, in_specs=[vmem] * n_in + [pl.BlockSpec(memory_space=...  21.6 us
    dot_general x5, matrix products, to_abs(): lax.dot_general(value, turn32, (((1,), (1,)), ((), ())), precision=HIGHEST)  9.24 us
  transfers between devices with their start and end apart: 71, of which 28 were waited for; matrix products, arithmetic and copies ran while one was open for 15% of the time, Pallas kernels for 27%

commit v1 on v0

--- a/solution.py
+++ b/solution.py
@@ -802,13 +802,13 @@
         rows_f0 = net.swap_out(stash)
         g_lang, sums7, bias1, stash = att_backward(g_lang, lang1, mask1, rows3(7), kept1, full["a1"], heads_here, groups)
         rows_a1 = net.swap_out(stash)
-        lang_out = to_abs(lang_out)
-        part0 = net.fold_wide([("d", rows_f0), ("u", rows_f0)], [sums7, lang_out])
+        part0 = net.fold_wide([("d", rows_f0), ("u", rows_f0)], [sums7])
         full.update(net.swap_late(pair3, net.gate(part0)))
         first = ffn_both(visn2, to_rel(visn_cot), bias_ff[1], rows3(18), full["u1"], full["d1"], groups, net.gate(part0))
         visn_out, g_visn, sums18, bias_visn, stash = tie(first, net.landed(part0))
         rows_f1 = net.swap_out(stash)
-        part0 = net.merge(part0, sums18)
+        lang_out, visn_out = to_abs(lang_out), to_abs(first[0])
+        part0 = net.merge(part0, [sums18, lang_out, visn_out])
         held0 = net.over_z(part0)
         part1 = net.send(net.fold([("d", rows_f1), ("u", rows_f1)], net.gate(part0)))
         first = att_backward(g_visn, visn1, mask2, rows3(12), kept2, full["a2"], heads_here, groups, net.gate(part1))
@@ -831,7 +831,7 @@
         by_heads = lax.dot_general(
             jnp.concatenate([bias0, bias1, bias2], axis=0), turn_heads, (((1,), (1,)), ((), ())), precision=HIGHEST
         )
-        lang_grad, visn_grad, visn_out = to_abs(g_both[:n_lang]), to_abs(g_both[n_lang:]), to_abs(visn_out)
+        lang_grad, visn_grad = to_abs(g_both[:n_lang]), to_abs(g_both[n_lang:])
 
         whole = []
         for b in range(3):
@@ -839,7 +839,7 @@
         by_rows = jnp.concatenate(whole + [by_rows[15:]], axis=0)
         bias_all = by_piece(jnp.stack([bias_lang, bias_visn]))
         sums = net.first_totals(tie(jnp.concatenate([by_rows, bias_all.reshape(-1, width)], axis=0), net.gate(part3)))
-        part2, part3 = net.merge_and_bump(part2, part3, after=listed(sums, held0, lang_grad, visn_grad, visn_out))
+        part2, part3 = net.merge_and_bump(part2, part3, after=listed(sums, held0, lang_grad, visn_grad))
         part3 = net.go(part3)
         held2 = net.over_z(part2)
         share0, share1, share2 = net.rest(held0), net.rest(held1), net.rest(held2)

time: 390 us -> 391 us (level)
    unnamed x246 -> x240, local copies, waits for them, and re-layouts: 38.9 us -> 37.9 us
  transfers between devices with their start and end apart: 71 -> 71, of which waited for: 28 -> 27; matrix products, arithmetic and copies ran while one was open for 15% -> 15% of each run, Pallas kernels for 27% -> 27%
where the time goes in v1:
time: 391 us; the launch traced here: 386 us
  waiting for transfers between devices  109 us (28%)
  Pallas kernels  107 us (27%)
  local copies, waits for them, and re-layouts  64.1 us (16%)
  starting transfers between devices  55 us (14%)
  matrix products  18.8 us (5%)
  between operations  16 us (4%)
  other arithmetic  15.7 us (4%)
    ppermute x65, waiting for transfers between devices, swap(): return lax.ppermute(value, axis, [(i, i ^ mask) for i in range(size)])  102 us
    pallas_call x8, Pallas kernels, call(): pl.pallas_call(body, grid=(1,), out_shape=tuple(outs), scratch_shapes=lis...  77.9 us
    ppermute x65, starting transfers between devices, swap(): return lax.ppermute(value, axis, [(i, i ^ mask) for i in range(size)])  53.9 us
    unnamed x240, local copies, waits for them, and re-layouts  37.9 us
    pallas_call x9, Pallas kernels, small(): pl.pallas_call(body, in_specs=[vmem] * n_in + [pl.BlockSpec(memory_space=...  22 us
    dot_general x5, matrix products, to_abs(): lax.dot_general(value, turn32, (((1,), (1,)), ((), ())), precision=HIGHEST)  9.98 us
  transfers between devices with their start and end apart: 71, of which 27 were waited for; matrix products, arithmetic and copies ran while one was open for 15% of the time, Pallas kernels for 27%

profile of v1, /device:TPU:0, one launch (start us, length us, event | category | flops | bytes accessed | tf_op | source)
XLA Modules:
  0.0 386.2 jit_solution(4748654616561405746)
XLA Ops:
  10.8 5.0 %collective-permute-start.2 = (bf16[1,96,768]{2,1,0:T(8,128)(2,1)}, bf16[1,96,768]{2,1,0:T(8,128)(2,1)S(1)}, u32[]{:S(2)}, u32[]{:S(2)}) collective-permute-start(bf16[1,96,768]{2,1,0:T(8,128)(2,1)} %bitcast.18), channel_id=1, source_target_pairs={{0,24},{4,28},{8,16},{12,20},{16,8},{20,12},{24,0},{28,4},{1,25},{... | collective-permute-start | bytes 442376 | tf_op jit(solution)/shard_map/ppermute | solution.py:142
  21.4 4.3 %collective-permute-done = bf16[1,96,768]{2,1,0:T(8,128)(2,1)} collective-permute-done((bf16[1,96,768]{2,1,0:T(8,128)(2,1)}, bf16[1,96,768]{2,1,0:T(8,128)(2,1)}, u32[]{:S(2)}, u32[]{:S(2)}) %collective-permute-start) | collective-permute-done | bytes 147488 | tf_op jit(solution)/shard_map/ppermute | solution.py:142
  36.0 8.5 %collective-permute-done.6.refs_8_.refs_12_ = bf16[4,1,96,768]{3,2,1,0:T(8,128)(2,1)} collective-permute-done((bf16[4,1,96,768]{3,2,1,0:T(8,128)(2,1)S(1)}, bf16[4,1,96,768]{3,2,1,0:T(8,128)(2,1)}, u32[]{:S(2)}, u32[]{:S(2)}) %collective-permute-start.6) | collective-permute-done | bytes 589856 | tf_op jit(solution)/shard_map/ppermute | solution.py:142
  50.7 6.8 %all-gather.7.cloned.1.call-done = bf16[8,96,768]{2,1,0:T(8,128)(2,1)} async-done(((bf16[2,96,768]{2,1,0:T(8,128)(2,1)}), bf16[8,96,768]{2,1,0:T(8,128)(2,1)}) %all-gather.7.cloned.1.call-update) | async-done | bytes 1179664 | tf_op jit(solution)/shard_map/all_gather | solution.py:181
  65.8 2.7 fusion.12.refs_0_.refs_1_
  73.2 11.8 %shard_map.470 = (f32[336,768]{1,0:T(8,128)S(1)}, f32[336,768]{1,0:T(8,128)S(1)}, f32[336,128]{1,0:T(8,128)S(1)}, bf16[4,336,768]{2,1,0:T(8,128)(2,1)S(1)}, bf16[4,336,256]{2,1,0:T(8,128)(2,1)S(1)}) custom-call(f32[336,768]{1,0:T(8,128)S(1)} %copy-done.104, f32[336,336]{1,0:T(8,128)S(1)} %copy-done.64, f32[2,768]{1,0:T(2,128)S(1)} %get-tuple-element.433.refs_2_, ...), custom_call_target="tpu_custom_call" | custom-call | flops 2358400000 | bytes 1024 | tf_op jit(solution)/shard_map/pallas_call | solution.py:663
  92.0 12.8 %collective-permute-done.15.refs_9_.refs_13_ = bf16[4,1,96,768]{3,2,1,0:T(8,128)(2,1)S(1)} collective-permute-done((bf16[4,1,96,768]{3,2,1,0:T(8,128)(2,1)S(1)}, bf16[4,1,96,768]{3,2,1,0:T(8,128)(2,1)S(1)}, u32[]{:S(2)}, u32[]{:S(2)}) %collective-permute-start.15) | collective-permute-done | bytes 589856 | tf_op jit(solution)/shard_map/ppermute | solution.py:142
  111.4 6.5 %shard_map.471 = (f32[120,768]{1,0:T(8,128)S(1)}, f32[120,768]{1,0:T(8,128)S(1)}, f32[120,128]{1,0:T(8,128)S(1)}, bf16[4,120,768]{2,1,0:T(8,128)(2,1)S(1)}, bf16[4,120,256]{2,1,0:T(8,128)(2,1)S(1)}) custom-call(f32[120,768]{1,0:T(8,128)S(1)} %slice.194.refs_0_.refs_1_, f32[120,120]{1,0:T(8,128)S(1)} %slice_convert_fusion.1.refs_1_.refs_2_, ...), custom_call_target="tpu_custom_call" | custom-call | flops 1408000000 | bytes 1024 | tf_op jit(solution)/shard_map/pallas_call | solution.py:663
  121.6 7.6 %shard_map.472 = (f32[216,768]{1,0:T(8,128)S(1)}, f32[216,768]{1,0:T(8,128)S(1)}, f32[216,128]{1,0:T(8,128)S(1)}, bf16[4,216,768]{2,1,0:T(8,128)(2,1)S(1)}, bf16[4,216,256]{2,1,0:T(8,128)(2,1)S(1)}) custom-call(f32[216,768]{1,0:T(8,128)S(1)} %slice.209.refs_0_.refs_1_, f32[216,216]{1,0:T(8,128)S(1)} %slice_convert_fusion.refs_1_.refs_2_, ...), custom_call_target="tpu_custom_call" | custom-call | flops 1830400000 | bytes 1024 | tf_op jit(solution)/shard_map/pallas_call | solution.py:663
  130.8 3.5 collective-permute-done.21.refs_8_.refs_16_
  140.3 10.3 %collective-permute-done.27.refs_17_ = bf16[4,1,96,768]{3,2,1,0:T(8,128)(2,1)} collective-permute-done((bf16[4,1,96,768]{3,2,1,0:T(8,128)(2,1)S(1)}, bf16[4,1,96,768]{3,2,1,0:T(8,128)(2,1)}, u32[]{:S(2)}, u32[]{:S(2)}) %collective-permute-start.27) | collective-permute-done | bytes 589856 | tf_op jit(solution)/shard_map/ppermute | solution.py:142
  156.9 3.0 fusion.52
  162.2 10.1 %shard_map.473 = (f32[120,768]{1,0:T(8,128)S(1)}, f32[120,768]{1,0:T(8,128)S(1)}, f32[8,768]{1,0:T(8,128)S(1)}, f32[4,768]{1,0:T(4,128)S(1)}, bf16[6,120,768]{2,...) custom-call(f32[120,768]{1,0:T(8,128)S(1)} %copy-done.73, bf16[120,768]{1,0:T(8,128)(2,1)S(1)} %copy-done.76, ...), custom_call_target="tpu_custom_call" | custom-call | flops 2068000000 | bytes 1024 | tf_op jit(solution)/shard_map/pallas_call | solution.py:663
  172.4 7.1 %shard_map.474 = (f32[120,768]{1,0:T(8,128)S(1)}, f32[8,768]{1,0:T(8,128)S(1)}, f32[2,768]{1,0:T(2,128)S(1)}, bf16[4,120,768]{2,1,0:T(8,128)(2,1)S(1)}, bf16[4,120,768]{2,1,0:T(8,128)(2,1)S(1)}) custom-call(f32[120,768]{1,0:T(8,128)S(1)} %get-tuple-element.234.refs_0_, f32[120,768]{1,0:T(8,128)S(1)} %copy-done.19, ...), custom_call_target="tpu_custom_call" | custom-call | flops 1895384576 | bytes 1024 | tf_op jit(solution)/shard_map/pallas_call | solution.py:663
  180.5 2.6 shard_map.475
  184.6 3.7 collective-permute-done.33.refs_16_.refs_17_
  193.8 9.8 %shard_map.476 = (f32[216,768]{1,0:T(8,128)S(1)}, f32[216,768]{1,0:T(8,128)S(1)}, f32[8,768]{1,0:T(8,128)S(1)}, f32[4,768]{1,0:T(4,128)S(1)}, bf16[6,216,768]{2,...) custom-call(f32[216,768]{1,0:T(8,128)S(1)} %copy-done.53, bf16[216,768]{1,0:T(8,128)(2,1)S(1)} %fusion.14.refs_1_, ...), custom_call_target="tpu_custom_call" | custom-call | flops 2490400000 | bytes 1024 | tf_op jit(solution)/shard_map/pallas_call | solution.py:663
  204.8 12.8 %collective-permute-done.37.refs_1_ = bf16[2,384,768]{2,1,0:T(8,128)(2,1)S(1)} collective-permute-done((bf16[2,384,768]{2,1,0:T(8,128)(2,1)S(1)}, bf16[2,384,768]{2,1,0:T(8,128)(2,1)S(1)}, u32[]{:S(2)}, u32[]{:S(2)}) %collective-permute-start.37) | collective-permute-done | bytes 1179680 | tf_op jit(solution)/shard_map/ppermute | solution.py:142
  227.8 4.8 %shard_map.478 = (bf16[2,384,768]{2,1,0:T(8,128)(2,1)S(1)}, bf16[2,384,768]{2,1,0:T(8,128)(2,1)S(1)}, bf16[2,384,768]{2,1,0:T(8,128)(2,1)S(1)}, bf16[384,768]{1,0:T(8,128)(2,1)S(1)}, bf16[384,768]{1,0:T(8,128)(2,1)S(1)}) custom-call(bf16[6,216,768]{2,1,0:T(8,128)(2,1)S(1)} %copy-done.38, bf16[6,216,768]{2,1,0:T(8,128)(2,1)} %collective-permute-done.39.refs_1_, ...), custom_call_target="tpu_custom_call" | custom-call | flops 660000000 | bytes 1024 | tf_op jit(solution)/shard_map/pallas_call | solution.py:584
  234.4 9.0 %shard_map.479 = (f32[216,768]{1,0:T(8,128)S(1)}, f32[8,768]{1,0:T(8,128)S(1)}, f32[2,768]{1,0:T(2,128)S(1)}, bf16[4,216,768]{2,1,0:T(8,128)(2,1)S(1)}, bf16[4,216,768]{2,1,0:T(8,128)(2,1)S(1)}) custom-call(f32[216,768]{1,0:T(8,128)S(1)} %copy-done.57, f32[216,768]{1,0:T(8,128)S(1)} %slice.209.refs_0_.refs_1_, f32[216,216]{1,0:T(8,128)S(1)} %copy-done.36, ...), custom_call_target="tpu_custom_call" | custom-call | flops 2707692288 | bytes 1024 | tf_op jit(solution)/shard_map/pallas_call | solution.py:663
  243.4 4.9 %collective-permute-done.40.refs_2_ = bf16[384,768]{1,0:T(8,128)(2,1)S(1)} collective-permute-done((bf16[384,768]{1,0:T(8,128)(2,1)S(1)}, bf16[384,768]{1,0:T(8,128)(2,1)S(1)}, u32[]{:S(2)}, u32[]{:S(2)}) %collective-permute-start.40) | collective-permute-done | bytes 589856 | tf_op jit(solution)/shard_map/ppermute | solution.py:142
  253.0 4.0 %shard_map.481 = (bf16[2,384,768]{2,1,0:T(8,128)(2,1)S(1)}, bf16[2,384,768]{2,1,0:T(8,128)(2,1)S(1)}, bf16[2,384,768]{2,1,0:T(8,128)(2,1)S(1)}, bf16[384,768]{1,0:T(8,128)(2,1)S(1)}, bf16[384,768]{1,0:T(8,128)(2,1)S(1)}) custom-call(bf16[4,120,768]{2,1,0:T(8,128)(2,1)S(1)} %copy-done.49, bf16[4,120,768]{2,1,0:T(8,128)(2,1)S(1)} %collective-permute-done.42.refs_1_, ...), custom_call_target="tpu_custom_call" | custom-call | flops 660000000 | bytes 1024 | tf_op jit(solution)/shard_map/pallas_call | solution.py:584
  260.4 16.0 %shard_map.482 = (f32[336,768]{1,0:T(8,128)S(1)}, f32[8,768]{1,0:T(8,128)S(1)}, f32[2,768]{1,0:T(2,128)S(1)}, bf16[4,336,768]{2,1,0:T(8,128)(2,1)S(1)}, bf16[4,336,768]{2,1,0:T(8,128)(2,1)S(1)}) custom-call(f32[336,768]{1,0:T(8,128)S(1)} %pad_maximum_fusion.refs_0_, f32[336,768]{1,0:T(8,128)S(1)} %copy-done.105, f32[336,336]{1,0:T(8,128)S(1)} %copy-done.65, ...), custom_call_target="tpu_custom_call" | custom-call | flops 3723076864 | bytes 1024 | tf_op jit(solution)/shard_map/pallas_call | solution.py:663
  279.7 11.5 %collective-permute-done.46.refs_5_ = bf16[384,768]{1,0:T(8,128)(2,1)S(1)} collective-permute-done((bf16[384,768]{1,0:T(8,128)(2,1)S(1)}, bf16[384,768]{1,0:T(8,128)(2,1)S(1)}, u32[]{:S(2)}, u32[]{:S(2)}) %collective-permute-start.46) | collective-permute-done | bytes 589856 | tf_op jit(solution)/shard_map/ppermute | solution.py:142
  302.7 5.1 %shard_map.484 = (bf16[1,384,768]{2,1,0:T(8,128)(2,1)S(1)}, bf16[1,384,768]{2,1,0:T(8,128)(2,1)S(1)}, bf16[1,384,768]{2,1,0:T(8,128)(2,1)S(1)}, bf16[384,384]{1,0:T(8,128)(2,1)}, bf16[384,384]{1,0:T(8,128)(2,1)S(1)}) custom-call(bf16[4,336,768]{2,1,0:T(8,128)(2,1)S(1)} %get-tuple-element.304.refs_0_, bf16[4,336,768]{2,1,0:T(8,128)(2,1)} %collective-permute-done.48.refs_1_, ...), custom_call_target="tpu_custom_call" | custom-call | flops 660000000 | bytes 1024 | tf_op jit(solution)/shard_map/pallas_call | solution.py:584
  310.9 2.3 fusion.3
  313.1 6.2 %collective-permute-done.52 = f32[29,768]{1,0:T(8,128)S(1)} collective-permute-done((f32[29,768]{1,0:T(8,128)S(1)}, f32[29,768]{1,0:T(8,128)S(1)}, u32[]{:S(2)}, u32[]{:S(2)}) %collective-permute-start.52) | collective-permute-done | bytes 89120 | tf_op jit(solution)/shard_map/ppermute | solution.py:142
  321.6 5.6 %collective-permute-done.53 = f32[29,768]{1,0:T(8,128)S(1)} collective-permute-done((f32[29,768]{1,0:T(8,128)S(1)}, f32[29,768]{1,0:T(8,128)S(1)}, u32[]{:S(2)}, u32[]{:S(2)}) %collective-permute-start.53) | collective-permute-done | bytes 89120 | tf_op jit(solution)/shard_map/ppermute | solution.py:142
  327.3 3.5 collective-permute-done.56.refs_5_
  331.8 2.4 shard_map.487
  344.0 2.5 collective-permute-done.49
  354.6 3.4 collective-permute-done.58
  (475 shorter events, 160.2 us)
Async XLA Ops:
  7.2 50.2 %all-gather.7.cloned.1.call-start = ((), (), s32[]{:S(2)}) async-start(), calls=%async_computation.6 | async-start | bytes 1474560 | tf_op jit(solution)/shard_map/all_gather | solution.py:181
  17.9 45.9 %collective-permute-start.30 = (bf16[96,768]{1,0:T(8,128)(2,1)S(1)}, bf16[96,768]{1,0:T(8,128)(2,1)}, u32[]{:S(2)}, u32[]{:S(2)}) collective-permute-start(bf16[96,768]{1,0:T(8,128)(2,1)S(1)} %get-tuple-element.215), channel_id=1, source_target_pairs={{0,4},{4,0},{8,12},{12,8},{16,20},{20,16},{24,28},{28,24},{1,5},{5... | collective-permute-start | bytes 442376 | tf_op jit(solution)/shard_map/ppermute | solution.py:142
  19.7 44.1 %collective-permute-start.29 = (bf16[96,768]{1,0:T(8,128)(2,1)}, bf16[96,768]{1,0:T(8,128)(2,1)}, u32[]{:S(2)}, u32[]{:S(2)}) collective-permute-start(bf16[96,768]{1,0:T(8,128)(2,1)} %get-tuple-element.217), channel_id=1, source_target_pairs={{0,2},{1,3},{2,0},{3,1},{4,6},{5,7},{6,4},{7,5},{8,10},{9,11},{10,... | collective-permute-start | bytes 442376 | tf_op jit(solution)/shard_map/ppermute | solution.py:142
  26.7 78.9 %all-gather.9.cloned.1.call-start = ((), (), s32[]{:S(2)}) async-start(), calls=%async_computation.7 | async-start | bytes 1474560 | tf_op jit(solution)/shard_map/all_gather | solution.py:181
  33.9 122.9 %all-gather.11.cloned.1.call-start = ((), (), s32[]{:S(2)}) async-start(), calls=%async_computation.8 | async-start | bytes 2949120 | tf_op jit(solution)/shard_map/all_gather | solution.py:192
  36.0 28.4 %collective-permute-start.4 = (bf16[4,1,96,768]{3,2,1,0:T(8,128)(2,1)S(1)}, bf16[4,1,96,768]{3,2,1,0:T(8,128)(2,1)}, u32[]{:S(2)}, u32[]{:S(2)}) collective-permute-start(bf16[4,1,96,768]{3,2,1,0:T(8,128)(2,1)S(1)} %bitcast_dynamic-update-slice_fusion.refs_4_.refs_8_), channel_id=1, source_target_pairs={{0,1},{1,0},{2,3},{3,2},{4,5},{5,4},{6,7},{7,6},{8,9},{9,8},{10,11... | collective-permute-start | bytes 1769480 | tf_op jit(solution)/shard_map/ppermute | solution.py:142
  57.5 31.9 %collective-permute-start.14 = (bf16[4,2,96,768]{3,2,1,0:T(8,128)(2,1)}, bf16[4,2,96,768]{3,2,1,0:T(8,128)(2,1)S(1)}, u32[]{:S(2)}, u32[]{:S(2)}) collective-permute-start(bf16[4,2,96,768]{3,2,1,0:T(8,128)(2,1)} %bitcast.134), channel_id=1, source_target_pairs={{0,2},{1,3},{2,0},{3,1},{4,6},{5,7},{6,4},{7,5},{8,10},{9,11},{10,... | collective-permute-start | bytes 3538952 | tf_op jit(solution)/shard_map/ppermute | solution.py:142
  58.9 30.4 %collective-permute-start.11 = (bf16[4,2,96,768]{3,2,1,0:T(8,128)(2,1)}, bf16[4,2,96,768]{3,2,1,0:T(8,128)(2,1)S(1)}, u32[]{:S(2)}, u32[]{:S(2)}) collective-permute-start(bf16[4,2,96,768]{3,2,1,0:T(8,128)(2,1)} %bitcast.135), channel_id=1, source_target_pairs={{0,4},{4,0},{8,12},{12,8},{16,20},{20,16},{24,28},{28,24},{1,5},{5... | collective-permute-start | bytes 3538952 | tf_op jit(solution)/shard_map/ppermute | solution.py:142
  70.5 35.1 %collective-permute-start.12 = (bf16[4,2,96,768]{3,2,1,0:T(8,128)(2,1)}, bf16[4,2,96,768]{3,2,1,0:T(8,128)(2,1)}, u32[]{:S(2)}, u32[]{:S(2)}) collective-permute-start(bf16[4,2,96,768]{3,2,1,0:T(8,128)(2,1)} %bitcast.136), channel_id=1, source_target_pairs={{0,1},{1,0},{2,3},{3,2},{4,5},{5,4},{6,7},{7,6},{8,9},{9,8},{10,11... | collective-permute-start | bytes 3538952 | tf_op jit(solution)/shard_map/ppermute | solution.py:142
  89.1 238.1 %reduce-scatter.6.cloned.1.call-start = ((), (), s32[]{:S(2)}) async-start(), calls=%async_computation.4 | async-start | bytes 2949120 | tf_op jit(solution)/shard_map/reduce_scatter | solution.py:284
  91.5 19.9 %collective-permute-start.16 = (bf16[4,2,96,768]{3,2,1,0:T(8,128)(2,1)S(1)}, bf16[4,2,96,768]{3,2,1,0:T(8,128)(2,1)}, u32[]{:S(2)}, u32[]{:S(2)}) collective-permute-start(bf16[4,2,96,768]{3,2,1,0:T(8,128)(2,1)S(1)} %collective-permute-done.14.refs_8_.refs_12_), channel_id=1, source_target_pairs={{0,1},{1,0},{2,3},{3,2},{4,5},{5,4},{6,7},{7,6},{8,9},{9,8},{10,11... | collective-permute-start | bytes 3538952 | tf_op jit(solution)/shard_map/ppermute | solution.py:142
  91.5 19.9 %collective-permute-start.13 = (bf16[4,2,96,768]{3,2,1,0:T(8,128)(2,1)S(1)}, bf16[4,2,96,768]{3,2,1,0:T(8,128)(2,1)}, u32[]{:S(2)}, u32[]{:S(2)}) collective-permute-start(bf16[4,2,96,768]{3,2,1,0:T(8,128)(2,1)S(1)} %collective-permute-done.11.refs_5_.refs_9_), channel_id=1, source_target_pairs={{0,1},{1,0},{2,3},{3,2},{4,5},{5,4},{6,7},{7,6},{8,9},{9,8},{10,11... | collective-permute-start | bytes 3538952 | tf_op jit(solution)/shard_map/ppermute | solution.py:142
  105.6 28.7 %collective-permute-start.21 = (bf16[4,2,96,768]{3,2,1,0:T(8,128)(2,1)}, bf16[4,2,96,768]{3,2,1,0:T(8,128)(2,1)}, u32[]{:S(2)}, u32[]{:S(2)}) collective-permute-start(bf16[4,2,96,768]{3,2,1,0:T(8,128)(2,1)} %bitcast.41.refs_4_.refs_12_), channel_id=1, source_target_pairs={{0,2},{1,3},{2,0},{3,1},{4,6},{5,7},{6,4},{7,5},{8,10},{9,11},{10,... | collective-permute-start | bytes 3538952 | tf_op jit(solution)/shard_map/ppermute | solution.py:142
  106.3 28.3 %collective-permute-start.18 = (bf16[4,2,96,768]{3,2,1,0:T(8,128)(2,1)}, bf16[4,2,96,768]{3,2,1,0:T(8,128)(2,1)}, u32[]{:S(2)}, u32[]{:S(2)}) collective-permute-start(bf16[4,2,96,768]{3,2,1,0:T(8,128)(2,1)} %bitcast.41.refs_4_.refs_12_), channel_id=1, source_target_pairs={{0,4},{4,0},{8,12},{12,8},{16,20},{20,16},{24,28},{28,24},{1,5},{5... | collective-permute-start | bytes 3538952 | tf_op jit(solution)/shard_map/ppermute | solution.py:142
  139.7 20.1 %collective-permute-start.19 = (bf16[4,2,96,768]{3,2,1,0:T(8,128)(2,1)}, bf16[4,2,96,768]{3,2,1,0:T(8,128)(2,1)}, u32[]{:S(2)}, u32[]{:S(2)}) collective-permute-start(bf16[4,2,96,768]{3,2,1,0:T(8,128)(2,1)} %bitcast.41.refs_4_.refs_12_), channel_id=1, source_target_pairs={{0,1},{1,0},{2,3},{3,2},{4,5},{5,4},{6,7},{7,6},{8,9},{9,8},{10,11... | collective-permute-start | bytes 3538952 | tf_op jit(solution)/shard_map/ppermute | solution.py:142
  139.7 22.3 %collective-permute-start.25 = (bf16[4,2,96,768]{3,2,1,0:T(8,128)(2,1)}, bf16[4,2,96,768]{3,2,1,0:T(8,128)(2,1)}, u32[]{:S(2)}, u32[]{:S(2)}) collective-permute-start(bf16[4,2,96,768]{3,2,1,0:T(8,128)(2,1)} %collective-permute-done.21.refs_8_.refs_16_), channel_id=1, source_target_pairs={{0,1},{1,0},{2,3},{3,2},{4,5},{5,4},{6,7},{7,6},{8,9},{9,8},{10,11... | collective-permute-start | bytes 3538952 | tf_op jit(solution)/shard_map/ppermute | solution.py:142
  140.3 21.8 %collective-permute-start.20 = (bf16[4,2,96,768]{3,2,1,0:T(8,128)(2,1)}, bf16[4,2,96,768]{3,2,1,0:T(8,128)(2,1)}, u32[]{:S(2)}, u32[]{:S(2)}) collective-permute-start(bf16[4,2,96,768]{3,2,1,0:T(8,128)(2,1)} %collective-permute-done.18.refs_5_.refs_13_), channel_id=1, source_target_pairs={{0,1},{1,0},{2,3},{3,2},{4,5},{5,4},{6,7},{7,6},{8,9},{9,8},{10,11... | collective-permute-start | bytes 3538952 | tf_op jit(solution)/shard_map/ppermute | solution.py:142
  156.8 34.8 %collective-permute-start.32 = (bf16[4,4,96,768]{3,2,1,0:T(8,128)(2,1)}, bf16[4,4,96,768]{3,2,1,0:T(8,128)(2,1)S(1)}, u32[]{:S(2)}, u32[]{:S(2)}) collective-permute-start(bf16[4,4,96,768]{3,2,1,0:T(8,128)(2,1)} %bitcast.128), channel_id=1, source_target_pairs={{0,1},{1,0},{2,3},{3,2},{4,5},{5,4},{6,7},{7,6},{8,9},{9,8},{10,11... | collective-permute-start | bytes 7077896 | tf_op jit(solution)/shard_map/ppermute | solution.py:142
  159.9 28.5 %collective-permute-start.33 = (bf16[4,2,96,768]{3,2,1,0:T(8,128)(2,1)}, bf16[4,2,96,768]{3,2,1,0:T(8,128)(2,1)S(1)}, u32[]{:S(2)}, u32[]{:S(2)}) collective-permute-start(bf16[4,2,96,768]{3,2,1,0:T(8,128)(2,1)} %get-tuple-element.401), channel_id=1, source_target_pairs={{0,2},{1,3},{2,0},{3,1},{4,6},{5,7},{6,4},{7,5},{8,10},{9,11},{10,... | collective-permute-start | bytes 3538952 | tf_op jit(solution)/shard_map/ppermute | solution.py:142
  161.2 28.0 %collective-permute-start.31 = (bf16[4,2,96,768]{3,2,1,0:T(8,128)(2,1)S(1)}, bf16[4,2,96,768]{3,2,1,0:T(8,128)(2,1)S(1)}, u32[]{:S(2)}, u32[]{:S(2)}) collective-permute-start(bf16[4,2,96,768]{3,2,1,0:T(8,128)(2,1)S(1)} %get-tuple-element.402), channel_id=1, source_target_pairs={{0,4},{4,0},{8,12},{12,8},{16,20},{20,16},{24,28},{28,24},{1,5},{5... | collective-permute-start | bytes 3538952 | tf_op jit(solution)/shard_map/ppermute | solution.py:142
  189.7 27.9 %collective-permute-start.37 = (bf16[2,384,768]{2,1,0:T(8,128)(2,1)S(1)}, bf16[2,384,768]{2,1,0:T(8,128)(2,1)S(1)}, u32[]{:S(2)}, u32[]{:S(2)}) collective-permute-start(bf16[2,384,768]{2,1,0:T(8,128)(2,1)S(1)} %get-tuple-element.250), channel_id=1, source_target_pairs={{0,4},{4,0},{8,12},{12,8},{16,20},{20,16},{24,28},{28,24},{1,5},{5... | collective-permute-start | bytes 3538952 | tf_op jit(solution)/shard_map/ppermute | solution.py:142
  190.3 27.6 %collective-permute-start.38 = (bf16[2,384,768]{2,1,0:T(8,128)(2,1)S(1)}, bf16[2,384,768]{2,1,0:T(8,128)(2,1)S(1)}, u32[]{:S(2)}, u32[]{:S(2)}) collective-permute-start(bf16[2,384,768]{2,1,0:T(8,128)(2,1)S(1)} %get-tuple-element.251), channel_id=1, source_target_pairs={{0,2},{1,3},{2,0},{3,1},{4,6},{5,7},{6,4},{7,5},{8,10},{9,11},{10,... | collective-permute-start | bytes 3538952 | tf_op jit(solution)/shard_map/ppermute | solution.py:142
  224.3 126.5 %reduce-scatter.4.cloned.1.call-start = ((), (), s32[]{:S(2)}) async-start(), calls=%async_computation.3 | async-start | bytes 1474560 | tf_op jit(solution)/shard_map/reduce_scatter | solution.py:284
  249.3 29.4 %collective-permute-start.44 = (bf16[2,384,768]{2,1,0:T(8,128)(2,1)S(1)}, bf16[2,384,768]{2,1,0:T(8,128)(2,1)S(1)}, u32[]{:S(2)}, u32[]{:S(2)}) collective-permute-start(bf16[2,384,768]{2,1,0:T(8,128)(2,1)S(1)} %get-tuple-element.275.refs_4_), channel_id=1, source_target_pairs={{0,4},{4,0},{8,12},{12,8},{16,20},{20,16},{24,28},{28,24},{1,5},{5... | collective-permute-start | bytes 3538952 | tf_op jit(solution)/shard_map/ppermute | solution.py:142
  250.8 28.9 %collective-permute-start.45 = (bf16[2,384,768]{2,1,0:T(8,128)(2,1)S(1)}, bf16[2,384,768]{2,1,0:T(8,128)(2,1)S(1)}, u32[]{:S(2)}, u32[]{:S(2)}) collective-permute-start(bf16[2,384,768]{2,1,0:T(8,128)(2,1)S(1)} %get-tuple-element.293), channel_id=1, source_target_pairs={{0,2},{1,3},{2,0},{3,1},{4,6},{5,7},{6,4},{7,5},{8,10},{9,11},{10,... | collective-permute-start | bytes 3538952 | tf_op jit(solution)/shard_map/ppermute | solution.py:142
  257.0 34.1 %collective-permute-start.46 = (bf16[384,768]{1,0:T(8,128)(2,1)S(1)}, bf16[384,768]{1,0:T(8,128)(2,1)S(1)}, u32[]{:S(2)}, u32[]{:S(2)}) collective-permute-start(bf16[384,768]{1,0:T(8,128)(2,1)S(1)} %get-tuple-element.300), channel_id=1, source_target_pairs={{0,2},{1,3},{2,0},{3,1},{4,6},{5,7},{6,4},{7,5},{8,10},{9,11},{10,... | collective-permute-start | bytes 1769480 | tf_op jit(solution)/shard_map/ppermute | solution.py:142
  258.7 32.4 %collective-permute-start.47 = (bf16[384,768]{1,0:T(8,128)(2,1)S(1)}, bf16[384,768]{1,0:T(8,128)(2,1)S(1)}, u32[]{:S(2)}, u32[]{:S(2)}) collective-permute-start(bf16[384,768]{1,0:T(8,128)(2,1)S(1)} %get-tuple-element.301), channel_id=1, source_target_pairs={{0,4},{4,0},{8,12},{12,8},{16,20},{20,16},{24,28},{28,24},{1,5},{5... | collective-permute-start | bytes 1769480 | tf_op jit(solution)/shard_map/ppermute | solution.py:142
  295.2 75.1 %reduce-scatter.8.cloned.1.call-start = ((), (), s32[]{:S(2)}) async-start(), calls=%async_computation.5 | async-start | bytes 1474560 | tf_op jit(solution)/shard_map/reduce_scatter | solution.py:284
  296.0 31.3 %collective-permute-start.54 = (bf16[2,384,768]{2,1,0:T(8,128)(2,1)}, bf16[2,384,768]{2,1,0:T(8,128)(2,1)}, u32[]{:S(2)}, u32[]{:S(2)}) collective-permute-start(bf16[2,384,768]{2,1,0:T(8,128)(2,1)} %copy-done.45), channel_id=1, source_target_pairs={{0,4},{4,0},{8,12},{12,8},{16,20},{20,16},{24,28},{28,24},{1,5},{5... | collective-permute-start | bytes 3538952 | tf_op jit(solution)/shard_map/ppermute | solution.py:142
  296.6 30.6 %collective-permute-start.55 = (bf16[2,384,768]{2,1,0:T(8,128)(2,1)}, bf16[2,384,768]{2,1,0:T(8,128)(2,1)}, u32[]{:S(2)}, u32[]{:S(2)}) collective-permute-start(bf16[2,384,768]{2,1,0:T(8,128)(2,1)} %copy-done.93), channel_id=1, source_target_pairs={{0,2},{1,3},{2,0},{3,1},{4,6},{5,7},{6,4},{7,5},{8,10},{9,11},{10,... | collective-permute-start | bytes 3538952 | tf_op jit(solution)/shard_map/ppermute | solution.py:142
  307.9 22.8 %collective-permute-start.56 = (bf16[384,384]{1,0:T(8,128)(2,1)}, bf16[384,384]{1,0:T(8,128)(2,1)S(1)}, u32[]{:S(2)}, u32[]{:S(2)}) collective-permute-start(bf16[384,384]{1,0:T(8,128)(2,1)} %get-tuple-element.338), channel_id=1, source_target_pairs={{0,2},{1,3},{2,0},{3,1},{4,6},{5,7},{6,4},{7,5},{8,10},{9,11},{10,... | collective-permute-start | bytes 884744 | tf_op jit(solution)/shard_map/ppermute | solution.py:142
  308.3 22.4 %collective-permute-start.57 = (bf16[384,384]{1,0:T(8,128)(2,1)S(1)}, bf16[384,384]{1,0:T(8,128)(2,1)S(1)}, u32[]{:S(2)}, u32[]{:S(2)}) collective-permute-start(bf16[384,384]{1,0:T(8,128)(2,1)S(1)} %get-tuple-element.339), channel_id=1, source_target_pairs={{0,4},{4,0},{8,12},{12,8},{16,20},{20,16},{24,28},{28,24},{1,5},{5... | collective-permute-start | bytes 884744 | tf_op jit(solution)/shard_map/ppermute | solution.py:142
  (158 other events, 1341.3 us)
Sparse Core Ops, SparseCore 0:
  26.9 30.5 all-gather.6
  59.6 29.5 all-gather.8
  91.3 49.5 all-gather.10
  224.4 46.5 reduce-scatter.5
  295.3 31.3 reduce-scatter.3
  337.0 28.1 reduce-scatter.7
